TPU v7x, 32 devices: a whole 2x2x4 slice. The times are simulated.
32 devices in a mesh: dp: 4 (over y, core), fsdp: 8 (over z, x).
Axes of the slice: x: 2, y: 2, z: 4, core: 2. Of those that a mesh axis runs over, the one named last changes fastest.
Arguments:
- images: bfloat16 [32, 26, 38, 768], P(('dp', 'fsdp')), may hold values from -6 to 6
- grad_out: bfloat16 [32, 26, 38, 768], P(('dp', 'fsdp')), may hold values from -6 to 6
- box_rows: int32 [32, 300, 2], P(('dp', 'fsdp')), may hold values from 0 to 26
- box_cols: int32 [32, 300, 2], P(('dp', 'fsdp')), may hold values from 0 to 38
- box_valid: int32 [32, 300], P(('dp', 'fsdp')), may hold values 0 or 1
- box_count: int32 [32], P(('dp', 'fsdp')), may hold values from 1 to 300
- in_weight: bfloat16 [768, 2304], P(('dp', 'fsdp')), may hold values from -0.21875 to 0.21875
- query_bias: bfloat16 [768], P(('dp', 'fsdp')), may hold values from -2 to 2
- value_bias: bfloat16 [768], P(('dp', 'fsdp')), may hold values from -2 to 2
- out_weight: bfloat16 [768, 768], P(('dp', 'fsdp')), may hold values from -1.75 to 1.75
- out_bias: bfloat16 [768], P(('dp', 'fsdp')), may hold values from -2 to 2
- first_gain: bfloat16 [768], P(('dp', 'fsdp')), may hold values from 0.099609375 to 1.8984375
- first_shift: bfloat16 [768], P(('dp', 'fsdp')), may hold values from -2 to 2
- second_gain: bfloat16 [768], P(('dp', 'fsdp')), may hold values from 0.099609375 to 1.8984375
- second_shift: bfloat16 [768], P(('dp', 'fsdp')), may hold values from -2 to 2
- up_weight: bfloat16 [768, 3072], P(('dp', 'fsdp')), may hold values from -0.21875 to 0.21875
- up_bias: bfloat16 [3072], P(('dp', 'fsdp')), may hold values from -2 to 2
- down_weight: bfloat16 [3072, 768], P(('dp', 'fsdp')), may hold values from -0.109375 to 0.109375
- down_bias: bfloat16 [768], P(('dp', 'fsdp')), may hold values from -2 to 2
- row_table: bfloat16 [27, 64], replicated, may hold values from -1 to 1
- col_table: bfloat16 [27, 64], replicated, may hold values from -1 to 1
Outputs:
- block_out: bfloat16 [32, 26, 38, 768], P(('dp', 'fsdp'))
- image_grad: bfloat16 [32, 26, 38, 768], P(('dp', 'fsdp'))
- in_weight_grad: float32 [768, 2304], P(('dp', 'fsdp'))
- query_bias_grad: float32 [768], P(('dp', 'fsdp'))
- value_bias_grad: float32 [768], P(('dp', 'fsdp'))
- out_weight_grad: float32 [768, 768], P(('dp', 'fsdp'))
- out_bias_grad: float32 [768], P(('dp', 'fsdp'))
- first_gain_grad: float32 [768], P(('dp', 'fsdp'))
- first_shift_grad: float32 [768], P(('dp', 'fsdp'))
- second_gain_grad: float32 [768], P(('dp', 'fsdp'))
- second_shift_grad: float32 [768], P(('dp', 'fsdp'))
- up_weight_grad: float32 [768, 3072], P(('dp', 'fsdp'))
- up_bias_grad: float32 [3072], P(('dp', 'fsdp'))
- down_weight_grad: float32 [3072, 768], P(('dp', 'fsdp'))
- down_bias_grad: float32 [768], P(('dp', 'fsdp'))
- row_table_grad: float32 [27, 64], replicated
- col_table_grad: float32 [27, 64], replicated
All inputs are finite; a program needn't handle non-finite values. No bound on the sum of `box_valid` on one device may be relied on, other than what follows from the above.
Results may differ from a plain program's by a relative error of at most 0.013.
Values may be sent and summed in bfloat16 or wider, within the bound.
No kernel may reach another device: no remote copies, remote signals or barrier semaphores. Data moves between devices by JAX's collectives and lax.ppermute only.
A program may use at most 256 MiB of HBM per device.

v0:
```python
import functools

import jax
import jax.numpy as jnp
import numpy as np
from jax import lax
from jax.experimental import pallas as pl
from jax.experimental.pallas import tpu as pltpu
from jax.sharding import PartitionSpec as P

D = 768
HEADS = 12
HD = 64
FF = 3072
WIN = 14
GH = 26
GW = 38
NBOX = 300
ACROSS = 3
WINDOWS = 6
LINE = 16
TOK = WIN * LINE
REAL = GH * GW
DENSE = 992
HALF = DENSE // 2
PAIRS = HEADS // 2
STARTS = (0, 14, 28)
WIDTHS = (14, 14, 10)
CHUNK = 768
CALLS = (2, 4)
SPLITS = ((0, 256), (256, 256), (512, 256), (768, 224))
epsilon = 1e-06
f32 = jnp.float32
bf16 = jnp.bfloat16
LIMIT = 60 * 1024 * 1024


def dot(a, b):
    return lax.dot_general(a, b, (((1,), (0,)), ((), ())), preferred_element_type=f32)


def dot_bt(a, b):
    return lax.dot_general(a, b, (((1,), (1,)), ((), ())), preferred_element_type=f32)


def dot_at(a, b):
    return lax.dot_general(a, b, (((0,), (0,)), ((), ())), preferred_element_type=f32)


def unit_of(x):
    center = x - jnp.mean(x, axis=-1, keepdims=True)
    inverse = lax.rsqrt(jnp.mean(center * center, axis=-1, keepdims=True) + epsilon)
    return center * inverse, inverse


def norm_back(grad, unit, inverse, gain):
    scaled = grad * gain
    return inverse * (
        scaled
        - jnp.mean(scaled, axis=-1, keepdims=True)
        - unit * jnp.mean(scaled * unit, axis=-1, keepdims=True)
    )


def place_of(row):
    return (row // WIN) * ACROSS, row % WIN


def spread_row(row, value, out_ref):
    first, place = place_of(row)
    for piece, (start, width) in enumerate(zip(STARTS, WIDTHS)):
        part = value[start : start + width]
        part = jnp.concatenate([part, jnp.zeros((LINE - width, part.shape[1]), part.dtype)], axis=0)
        out_ref[(first + piece) * WIN + place] = part.astype(out_ref.dtype)


def join_row(row, ref):
    first, place = place_of(row)
    return jnp.concatenate(
        [ref[(first + piece) * WIN + place].astype(f32)[:width] for piece, width in enumerate(WIDTHS)], axis=0
    )


def begin_kernel(img_ref, *refs):
    unit_ref, flag_ref = refs[-2:]
    flag_ref[0] = 0
    unit_ref[...] = jnp.zeros_like(unit_ref)
    for row in range(GH):
        unit, _ = unit_of(img_ref[row].astype(f32))
        spread_row(row, unit, unit_ref)


def pair_tables(row_table, col_table, entry_row, entry_col):
    parts = []
    for table, place in ((row_table, entry_row), (col_table, entry_col)):
        pieces = jnp.zeros((128, 128), f32)
        entries = lax.broadcasted_iota(jnp.int32, (2 * WIN - 1, 128), 0)
        lane = lane_iota((2 * WIN - 1, 128))
        row = lax.broadcasted_iota(jnp.int32, (128, 128), 0)
        for head in range(2):
            where = place(entries) + 32 * head
            pick = ((lane - where) % 64) == 0
            spread = dot_at(table, jnp.where(pick, 1.0, 0.0).astype(bf16))
            both = jnp.concatenate([spread, spread], axis=0)
            pieces = jnp.where((row < HD) == (head == 0), both, pieces)
        parts.append(pieces)
    return jnp.concatenate(parts, axis=1).astype(bf16)


def weight_kernel(count_ref, grad_ref, rows_ref, cols_ref, valid_ref, rowt_ref, colt_ref, *refs):
    cot_ref, upd_ref, table_ref, back_ref, flag_ref = refs[-5:]
    flag_ref[0] = 0
    table_ref[...] = pair_tables(rowt_ref[...], colt_ref[...], lambda e: 26 - e, lambda e: 29 - e)
    back_ref[...] = pair_tables(rowt_ref[...], colt_ref[...], lambda e: 26 - e, lambda e: 16 + e)
    slot = lax.broadcasted_iota(jnp.int32, (NBOX, 1), 0)
    live = (slot < count_ref[0]) & (valid_ref[...] == 1)
    rows = rows_ref[...]
    cols = cols_ref[...]
    top = jnp.minimum(rows[:, 0:1], rows[:, 1:2])
    low = jnp.maximum(rows[:, 0:1], rows[:, 1:2])
    left = jnp.minimum(cols[:, 0:1], cols[:, 1:2])
    right = jnp.maximum(cols[:, 0:1], cols[:, 1:2])
    grid_r = lax.broadcasted_iota(jnp.int32, (NBOX, GH), 1)
    grid_c = lax.broadcasted_iota(jnp.int32, (NBOX, GW), 1)
    in_rows = jnp.where((grid_r >= top) & (grid_r < low) & live, 1.0, 0.0)
    in_cols = jnp.where((grid_c >= left) & (grid_c < right), 1.0, 0.0)
    inside = dot_at(in_cols.astype(bf16), in_rows.astype(bf16))
    total = jnp.sum(jnp.where(live, 1.0, 0.0))
    weight = 1.0 + 2.0 * inside / jnp.maximum(total, 1.0)
    for row in range(GH):
        cot_ref[row * GW : (row + 1) * GW, :] = grad_ref[row].astype(f32) * weight[:, row : row + 1]
    cot_ref[REAL:, :] = jnp.zeros((DENSE - REAL, D), f32)
    upd_ref[...] = cot_ref[...].astype(bf16)


def lane_iota(shape):
    return lax.broadcasted_iota(jnp.int32, shape, len(shape) - 1)


def position_terms(queries, table):
    both = dot(queries, table)
    row_part = both[:, :128].reshape(WIN, LINE, 128)
    col_part = both[:, 128:].reshape(WIN, LINE, 128)
    lane = lane_iota((LINE, 128))
    local = lane % 32
    out = []
    for place in range(WIN):
        rolled_r = pltpu.roll(row_part[place], (place - 13) % 128, 1)
        rolled_c = pltpu.roll(col_part[place], 0, 1, stride=1, stride_axis=0)
        value = jnp.where(local < 16, rolled_r, rolled_c)
        high = value.astype(bf16).astype(f32)
        value = jnp.where(lane < 64, high, value - high)
        value = jnp.where(lane == 14, 1.0, value)
        out.append(value)
    return jnp.concatenate(out, axis=0).astype(bf16)


def keep_head(value, head):
    lane = lane_iota(value.shape)
    return jnp.where((lane < HD) == (head == 0), value, jnp.zeros_like(value))


def forward_kernel(places_ref, *refs):
    one_half, two_half, one_other, two_other, unit_ref, table_ref, hot_ref = refs[:7]
    tiles_ref, packed_ref, soft_ref, att_ref, branch_ref, vec_ref, one_ref, two_ref, sems = refs[7:]
    step = pl.program_id(0)

    @pl.when(step == 0)
    def _():
        core = places_ref[1]
        made = []
        for i, (half, whole_ref, place) in enumerate(
            [
                (one_half, one_ref, core),
                (two_half, two_ref, core),
                (one_other, one_ref, 1 - core),
                (two_other, two_ref, 1 - core),
            ]
        ):
            for y in range(2):
                here = pl.ds(pl.multiple_of((2 * y + place) * (D // 4), D // 4), D // 4)
                copy = pltpu.make_async_copy(half.at[y], whole_ref.at[here, :], sems.at[2 * i + y])
                copy.start()
                made.append(copy)
        for copy in made:
            copy.wait()
        vec_ref[...] = one_ref[:, :128].astype(f32).T[:16]

    window = step
    token = lax.broadcasted_iota(jnp.int32, (TOK, 1), 0)
    row_limit = jnp.where(window < ACROSS, WIN, GH - WIN)
    col_limit = jnp.where(window % ACROSS == ACROSS - 1, WIDTHS[2], WIN)
    valid = (token // LINE < row_limit) & (token % LINE < col_limit)
    tiles_ref[...] = (unit_ref[...] * vec_ref[3:4, :] + jnp.where(valid, vec_ref[4:5, :], 0.0)).astype(bf16)
    tiles = tiles_ref[...]
    packed_ref[:, :D] = (dot(tiles, one_ref[:, 128 : 128 + D]) + vec_ref[0:1, :]).astype(bf16)
    packed_ref[:, D : 2 * D] = dot(tiles, one_ref[:, 128 + D :]).astype(bf16)
    packed_ref[:, 2 * D :] = (dot(tiles, two_ref[:, :D]) + vec_ref[1:2, :]).astype(bf16)
    for pair in range(PAIRS):
        at = pair * 128
        queries = packed_ref[:, at : at + 128]
        keys = packed_ref[:, D + at : D + at + 128]
        values = packed_ref[:, 2 * D + at : 2 * D + at + 128]
        left = jnp.concatenate([queries, position_terms(queries, table_ref[...])], axis=1)
        parts = []
        for head in range(2):
            scaled = (keep_head(keys.astype(f32), head) * 0.125).astype(bf16)
            right = jnp.concatenate([scaled, hot_ref[head]], axis=1)
            scores = dot_bt(left, right)
            power = jnp.exp(scores - jnp.max(scores, axis=-1, keepdims=True))
            soft = (power * (1.0 / jnp.sum(power, axis=-1, keepdims=True))).astype(bf16)
            soft_ref[2 * pair + head] = soft
            parts.append(dot(soft, values))
        lane = lane_iota((TOK, 128))
        att_ref[:, at : at + 128] = jnp.where(lane < HD, parts[0], parts[1]).astype(bf16)
    branch_ref[...] = dot(att_ref[...], two_ref[:, D:]) + vec_ref[2:3, :]


def backward_kernel(packed_ref, soft_ref, att_ref, gbr_ref, two_ref, table_ref, hot_ref, *refs):
    gpacked_ref, gbias_ref, gtab_ref, flag_ref, gatt_ref = refs[-5:]

    @pl.when(pl.program_id(0) == 0)
    def _():
        flag_ref[0] = 0
        gbias_ref[...] = jnp.zeros_like(gbias_ref)
        gtab_ref[...] = jnp.zeros_like(gtab_ref)

    gatt_ref[...] = dot_bt(gbr_ref[...], two_ref[:, D:]).astype(bf16)
    lane = lane_iota((LINE, 128))
    local = lane % 32
    wide = lane_iota((TOK, 128))
    for pair in range(PAIRS):
        at = pair * 128
        queries = packed_ref[:, at : at + 128]
        keys = packed_ref[:, D + at : D + at + 128]
        values = packed_ref[:, 2 * D + at : 2 * D + at + 128]
        gatt = gatt_ref[:, at : at + 128]
        product = gatt.astype(f32) * att_ref[:, at : at + 128].astype(f32)
        left = []
        right = []
        gvalues = []
        gkeys = []
        turned_g = gatt.T
        turned_q = queries.T
        for head in range(2):
            soft = soft_ref[2 * pair + head]
            delta = jnp.sum(keep_head(product, head), axis=-1, keepdims=True)
            gprobs = dot_bt(gatt, keep_head(values.astype(f32), head).astype(bf16))
            gscores = (soft.astype(f32) * (gprobs - delta)).astype(bf16)
            scaled = (keep_head(keys.astype(f32), head) * 0.125).astype(bf16)
            left.append(gscores)
            right.append(jnp.concatenate([scaled, hot_ref[head]], axis=1))
            rows = slice(head * HD, (head + 1) * HD)
            gvalues.append(dot(turned_g[rows], soft))
            gkeys.append(dot(turned_q[rows], gscores))
        both = dot(left[0], right[0]) + dot(left[1], right[1])
        terms = both[:, 128:].reshape(WIN, LINE, 128)
        rolled = []
        for place in range(WIN):
            value = terms[place]
            high = value.astype(bf16).astype(f32)
            value = jnp.where(lane < 64, high, value - high)
            row_part = jnp.where(local < WIN, value, 0.0)
            col_part = jnp.where((local >= 16) & (local < 16 + WIN), value, 0.0)
            row_part = pltpu.roll(row_part, 13 - place, 1)
            col_part = pltpu.roll(col_part, 0, 1, stride=1, stride_axis=0)
            rolled.append(jnp.concatenate([row_part, col_part], axis=1))
        rolled = jnp.concatenate(rolled, axis=0).astype(bf16)
        gqueries = both[:, :128] + dot_bt(rolled, table_ref[...])
        gtab_ref[...] += dot_at(rolled, queries)
        gq = gqueries.astype(bf16)
        gk = (jnp.concatenate(gkeys, axis=0) * 0.125).astype(bf16).T
        gv = jnp.concatenate(gvalues, axis=0).astype(bf16).T
        gpacked_ref[:, at : at + 128] = gq
        gpacked_ref[:, D + at : D + at + 128] = gk
        gpacked_ref[:, 2 * D + at : 2 * D + at + 128] = gv
        gbias_ref[0:1, at : at + 128] += jnp.sum(gq.astype(f32), axis=0, keepdims=True)
        gbias_ref[1:2, at : at + 128] += jnp.sum(gv.astype(f32), axis=0, keepdims=True)


def halve(core, value, keep_ref, send_ref, at):
    size = value.shape[0] // 4

    def put(first, second):
        for y in range(2):
            first[y * size : (y + 1) * size, at] = value[2 * y * size : (2 * y + 1) * size]
            second[y * size : (y + 1) * size, at] = value[(2 * y + 1) * size : (2 * y + 2) * size]

    @pl.when(core == 0)
    def _():
        put(keep_ref, send_ref)

    @pl.when(core == 1)
    def _():
        put(send_ref, keep_ref)


def attention_weights_kernel(core_ref, sums1_ref, sums2_ref, gupb_ref, tiles_ref, *refs):
    keep_ref, send_ref, flag_ref, gpacked, sems = refs[-5:]
    count = len(CALLS)
    gpacked_refs, gbias_refs = refs[:count], refs[count : 2 * count]
    flag_ref[0] = 0
    made = []
    for part in range(3):
        columns = slice(part * D, (part + 1) * D)
        at = 0
        for i, (windows, ref) in enumerate(zip(CALLS, gpacked_refs)):
            target = gpacked.at[at : at + windows * TOK, columns]
            copy = pltpu.make_async_copy(ref.at[:, columns], target, sems.at[part * count + i])
            copy.start()
            made.append(copy)
            at += windows * TOK
    gbias = gbias_refs[0][...]
    for ref in gbias_refs[1:]:
        gbias += ref[...]
    rows = [gbias[:2], sums2_ref[2:3, :], sums1_ref[:2, :], sums2_ref[:2, :], sums2_ref[3:4, :], gupb_ref[:4, :]]
    rows = jnp.concatenate(rows + [jnp.zeros((116, D), f32)], axis=0)
    value = jnp.concatenate([rows.T, jnp.zeros((D, 128), f32)], axis=1).astype(bf16)
    halve(core_ref[0], value, keep_ref, send_ref, slice(3 * D, 3 * D + 256))
    turned = tiles_ref[...].T
    for part in range(3):
        for copy in made[part * count : (part + 1) * count]:
            copy.wait()
        columns = slice(part * D, (part + 1) * D)
        halve(core_ref[0], dot(turned, gpacked[:, columns]).astype(bf16), keep_ref, send_ref, columns)


def gelu_parts(hidden):
    size = jnp.abs(hidden)
    power = jnp.exp(hidden * hidden * -0.5)
    denominator = 1.0 + (0.3275911 * 0.7071067811865476) * size
    near = pl.reciprocal(denominator, approx=True)
    near = near * (2.0 - denominator * near)
    series = near * (
        0.254829592
        + near * (-0.284496736 + near * (1.421413741 + near * (-1.453152027 + near * 1.061405429)))
    )
    tail = 0.5 * series * power
    normal = jnp.where(hidden >= 0, 1.0 - tail, tail)
    return hidden * normal, normal + hidden * power * 0.3989422804014327


def middle_kernel(
    core_ref,
    img_ref,
    cot_any,
    gupd_any,
    vec_ref,
    up_ref,
    down_ref,
    *refs,
):
    branch_ref, att_any = refs[:2]
    out_ref, gbr_ref, gupk_ref, gups_ref, gdownk_ref, gdowns_ref, gupb_ref, sums_ref = refs[2:10]
    mid, normed, update, gnorm, active, ghidden, cot_ref, gupd_ref, att_ref, sems = refs[10:]
    step = pl.program_id(0)

    def copies():
        pairs = ((gupd_any, gupd_ref), (cot_any, cot_ref), (att_any, att_ref))
        return [pltpu.make_async_copy(*pair, sems.at[i]) for i, pair in enumerate(pairs)]

    gain = vec_ref[5:6, :]
    shift = vec_ref[6:7, :]

    @pl.when(step == 0)
    def _():
        for copy in copies():
            copy.start()
        for row in range(GH):
            mid[row * GW : (row + 1) * GW, :] = img_ref[row].astype(f32) + join_row(row, branch_ref)
        mid[REAL:, :] = jnp.zeros((DENSE - REAL, D), f32)
        update[...] = jnp.zeros_like(update)
        gnorm[...] = jnp.zeros_like(gnorm)

        def chunk(index, carry):
            here = pl.ds(pl.multiple_of(index * HALF, HALF), HALF)
            unit, _ = unit_of(mid[here, :])
            normed[here, :] = (unit * gain + shift).astype(bf16)
            return carry

        lax.fori_loop(0, DENSE // HALF, chunk, 0)
        copies()[0].wait()

    @pl.when(step < FF // CHUNK)
    def _():
        up_bias = vec_ref[pl.ds(8 + step, 1), :]
        for start, size in SPLITS:
            here = slice(start, start + size)
            hidden = dot(normed[here, :], up_ref[...]) + up_bias
            gactive = dot_bt(gupd_ref[here, :], down_ref[...])
            act, slope = gelu_parts(hidden)
            act = act.astype(bf16)
            gh = (gactive * slope).astype(bf16)
            active[here, :] = act
            ghidden[here, :] = gh
            update[here, :] += dot(act, down_ref[...])
            gnorm[here, :] += dot_bt(gh, up_ref[...])
        gupb_ref[pl.ds(step, 1), :] = jnp.sum(ghidden[...].astype(f32), axis=0, keepdims=True)
        gdown = dot_at(active[...], gupd_ref[...]).astype(bf16)
        halve(core_ref[0], gdown, gdownk_ref, gdowns_ref, slice(None))
        gup = dot_at(normed[...], ghidden[...]).astype(bf16)
        halve(core_ref[0], gup, gupk_ref, gups_ref, slice(None))

    @pl.when(step == FF // CHUNK)
    def _():
        for copy in copies()[1:]:
            copy.wait()
        down_bias = vec_ref[7:8, :]
        for row in range(GH):
            here = slice(row * GW, (row + 1) * GW)
            out_ref[row] = (mid[here, :] + update[here, :] + down_bias).astype(bf16)

        def chunk(index, carry):
            here = pl.ds(pl.multiple_of(index * HALF, HALF), HALF)
            unit, inverse = unit_of(mid[here, :])
            grad = gnorm[here, :]
            cot = cot_ref[here, :]
            result = cot + norm_back(grad, unit, inverse, gain)
            rounded = result.astype(bf16).astype(f32)
            update[here, :] = rounded
            gain_sum, shift_sum, branch_sum, bias_sum = carry
            return (
                gain_sum + jnp.sum((grad * unit).reshape(HALF // 8, 8, D), axis=0),
                shift_sum + jnp.sum(grad.reshape(HALF // 8, 8, D), axis=0),
                branch_sum + jnp.sum(rounded.reshape(HALF // 8, 8, D), axis=0),
                bias_sum + jnp.sum(cot.astype(bf16).astype(f32).reshape(HALF // 8, 8, D), axis=0),
            )

        zero = jnp.zeros((8, D), f32)
        sums = lax.fori_loop(0, DENSE // HALF, chunk, (zero,) * 4)
        sums_ref[...] = jnp.concatenate(
            [jnp.sum(s, axis=0, keepdims=True) for s in sums] + [jnp.zeros((4, D), f32)], axis=0
        )
        gbr_ref[...] = jnp.zeros_like(gbr_ref)
        for row in range(GH):
            spread_row(row, update[row * GW : (row + 1) * GW, :], gbr_ref)
        gout = dot_at(att_ref[...], gbr_ref[...].reshape(WINDOWS * TOK, D))
        halve(core_ref[0], gout.astype(bf16), gupk_ref, gups_ref, slice(None))


def end_kernel(img_ref, gbr_ref, one_ref, two_ref, vec_ref, *refs):
    count = len(CALLS)
    gpacked_refs, gtab_refs = refs[:count], refs[count : 2 * count]
    out_ref, sums_ref, tables_ref, flag_ref, gtiles, gpacked, img, gbr, sems = refs[-9:]
    flag_ref[0] = 0
    made = []
    at = 0
    for i, (windows, ref) in enumerate(zip(CALLS, gpacked_refs)):
        made.append(pltpu.make_async_copy(ref, gpacked.at[at : at + windows * TOK, :], sems.at[i]))
        at += windows * TOK
    made.append(pltpu.make_async_copy(img_ref, img, sems.at[count]))
    made.append(pltpu.make_async_copy(gbr_ref, gbr, sems.at[count + 1]))
    for copy in made:
        copy.start()
    gain = vec_ref[3:4, :]
    at = 0
    for windows, copy in zip(CALLS, made):
        copy.wait()
        here = slice(at * TOK, (at + windows) * TOK)
        value = dot_bt(gpacked[here, : 2 * D], one_ref[:, 128:]) + dot_bt(gpacked[here, 2 * D :], two_ref[:, :D])
        gtiles[at * WIN : (at + windows) * WIN] = value.reshape(windows * WIN, LINE, D)
        at += windows
    for copy in made[count:]:
        copy.wait()
    gain_sum = jnp.zeros((1, D), f32)
    shift_sum = jnp.zeros((1, D), f32)
    for row in range(GH):
        unit, inverse = unit_of(img[row].astype(f32))
        grad = join_row(row, gtiles)
        gain_sum += jnp.sum(grad * unit, axis=0, keepdims=True)
        shift_sum += jnp.sum(grad, axis=0, keepdims=True)
        out_ref[row] = (join_row(row, gbr) + norm_back(grad, unit, inverse, gain)).astype(bf16)
    sums_ref[...] = jnp.concatenate([gain_sum, shift_sum, jnp.zeros((6, D), f32)], axis=0)
    total = gtab_refs[0][...]
    for ref in gtab_refs[1:]:
        total += ref[...]
    entries = 2 * WIN - 1
    rows = total[:128]
    cols = jnp.concatenate([total[128 + 16 :], total[128 : 128 + 16]], axis=0)
    tables = []
    for part in (rows, cols):
        whole_part = jnp.zeros((entries, HD), f32)
        for group in range(4):
            lines = part[32 * group : 32 * group + entries]
            whole_part += lines[:, HD:] if group % 2 else lines[:, :HD]
        tables.append(whole_part)
    flipped = [tables[0][entries - 1 - i : entries - i] for i in range(entries)]
    tables = jnp.concatenate(flipped + [tables[1], jnp.zeros((10, HD), f32)], axis=0)
    tables_ref[...] = jnp.concatenate([tables, jnp.zeros((64, HD), f32)], axis=1)


def pack_kernel(eight_ref, upb_ref, weight_ref, out_ref):
    own = weight_ref.shape[0]
    flat = upb_ref[...].astype(f32)
    rows = [eight_ref[...].astype(f32)] + [flat[:, own * i : own * (i + 1)] for i in range(4)]
    rows = jnp.concatenate(rows, axis=0)
    rows = jnp.concatenate([rows, jnp.zeros((12, 128 - own), f32)], axis=1)
    square = jnp.concatenate([rows, jnp.zeros((116, 128), f32)], axis=0)
    out_ref[:, :128] = square.T[:own].astype(bf16)
    out_ref[:, 128:] = weight_ref[:, : 2 * D]


def regroup(value, own, back=False):
    count = value.shape[1] // (4 * own)
    parts = []
    for i in range(count if back else 4):
        for j in range(4 if back else count):
            at = (j * count + i) * own if back else (4 * j + i) * own
            parts.append(value[:, at : at + own])
    return jnp.concatenate(parts, axis=1)


def pack_feed_kernel(up_ref, down_ref, out_ref):
    own = up_ref.shape[0]
    out_ref[:, :FF] = regroup(up_ref[...].astype(f32), own).astype(bf16)
    for k in range(4):
        part = down_ref[...].astype(f32)[k * own : (k + 1) * own]
        out_ref[:, FF + k * D : FF + (k + 1) * D] = part.astype(bf16)


def unpack_feed_kernel(first, second, up_ref, out_ref, down_ref):
    own = up_ref.shape[0]
    up_ref[...] = regroup(first[:, :FF], own, back=True)
    out_ref[...] = first[:, FF:]
    for k in range(4):
        down_ref[k * own : (k + 1) * own, :] = second[:, k * D : (k + 1) * D]


def unpack_in_kernel(first, second, tables_ref, in_ref, *refs):
    entries = 2 * WIN - 1
    tables = jnp.sum(tables_ref[...], axis=0)
    refs[-2][...] = tables[:entries, :HD]
    refs[-1][...] = tables[entries : 2 * entries, :HD]
    half = first.shape[1]
    in_ref[:, :half] = first
    in_ref[:, half:] = second[:, : 3 * D - half]
    own = first.shape[0]
    square = jnp.concatenate([second[:, 3 * D - half : 3 * D - half + 128], jnp.zeros((128 - own, 128), f32)], axis=0)
    rows = square.T
    for i in range(8):
        refs[i][...] = rows[i : i + 1, :own]
    refs[8][...] = jnp.concatenate([rows[i : i + 1, :own] for i in range(8, 12)], axis=1)


def params(steps=0):
    return pltpu.CompilerParams(
        vmem_limit_bytes=LIMIT, dimension_semantics=("arbitrary",) * steps if steps else None
    )


VMEM = pl.BlockSpec(memory_space=pltpu.VMEM)
SMEM = pl.BlockSpec(memory_space=pltpu.SMEM)


def whole(shape):
    return pl.BlockSpec(shape, lambda i: (0,) * len(shape))


def shaped(shape, dtype):
    return jax.ShapeDtypeStruct(shape, dtype)


def pack_feed(up, down):
    own = up.shape[0]
    return pl.pallas_call(
        pack_feed_kernel,
        out_shape=shaped((own, 2 * FF), bf16),
        in_specs=[VMEM] * 2,
        out_specs=VMEM,
        compiler_params=params(),
        name="pack_feed",
    )(up, down)


FLAG = pl.BlockSpec(memory_space=pltpu.SMEM)
ANY = pl.BlockSpec(memory_space=pl.ANY)
flag_shape = jax.ShapeDtypeStruct((1,), jnp.int32)


def begin(images, before):
    return pl.pallas_call(
        begin_kernel,
        out_shape=(shaped((WINDOWS * WIN, LINE, D), f32), flag_shape),
        in_specs=[VMEM] + [ANY] * len(before),
        out_specs=(VMEM, FLAG),
        compiler_params=params(),
        cost_estimate=pl.CostEstimate(flops=30_000_000, bytes_accessed=6_000_000, transcendentals=0),
        name="begin",
    )(images, *before)


def weigh(count, grad_out, rows, cols, valid, row_table, col_table, before):
    return pl.pallas_call(
        weight_kernel,
        out_shape=(
            shaped((DENSE, D), f32),
            shaped((DENSE, D), bf16),
            shaped((128, 256), bf16),
            shaped((128, 256), bf16),
            flag_shape,
        ),
        in_specs=[SMEM] + [VMEM] * 6 + [ANY] * len(before),
        out_specs=(VMEM,) * 4 + (FLAG,),
        compiler_params=params(),
        cost_estimate=pl.CostEstimate(flops=30_000_000, bytes_accessed=6_000_000, transcendentals=0),
        name="weigh",
    )(count, grad_out, rows, cols, valid, row_table, col_table, *before)


def forward(places, halves, unit, table, hot):
    per = lambda *shape: pl.BlockSpec(shape, lambda i: (i,) + (0,) * (len(shape) - 1))
    return pl.pallas_call(
        forward_kernel,
        grid=(WINDOWS,),
        out_shape=(
            shaped((WINDOWS * TOK, D), bf16),
            shaped((WINDOWS * TOK, 3 * D), bf16),
            shaped((WINDOWS * HEADS, TOK, TOK), bf16),
            shaped((WINDOWS * TOK, D), bf16),
            shaped((WINDOWS * TOK, D), f32),
            shaped((16, D), f32),
            shaped((D, 128 + 2 * D), bf16),
            shaped((D, 2 * D), bf16),
        ),
        in_specs=[SMEM] + [ANY] * 4 + [per(TOK, D), whole((128, 256)), whole((2, TOK, 128))],
        out_specs=(
            per(TOK, D),
            per(TOK, 3 * D),
            per(HEADS, TOK, TOK),
            per(TOK, D),
            per(TOK, D),
            whole((16, D)),
            whole((D, 128 + 2 * D)),
            whole((D, 2 * D)),
        ),
        scratch_shapes=[pltpu.SemaphoreType.DMA((8,))],
        compiler_params=params(1),
        cost_estimate=pl.CostEstimate(flops=30_000_000_000, bytes_accessed=28_000_000, transcendentals=4_000_000),
        name="attend",
    )(places, *halves, unit, table, hot)


def middle(core, images, cot, gupd, vec, weights, branch, attended):
    steps = FF // CHUNK
    at = lambda i: jnp.minimum(i, steps - 1)
    return pl.pallas_call(
        middle_kernel,
        grid=(steps + 1,),
        out_shape=(
            shaped((GH, GW, D), bf16),
            shaped((WINDOWS * WIN, LINE, D), bf16),
            shaped((D // 2, FF + D), bf16),
            shaped((D // 2, FF + D), bf16),
            shaped((D // 2, FF), bf16),
            shaped((D // 2, FF), bf16),
            shaped((8, D), f32),
            shaped((8, D), f32),
        ),
        in_specs=[
            SMEM,
            whole((GH, GW, D)),
            ANY,
            ANY,
            whole((16, D)),
            pl.BlockSpec((D, CHUNK), lambda i: (0, at(i))),
            pl.BlockSpec((D, CHUNK), lambda i: (0, steps + at(i))),
        ]
        + [whole((WINDOWS * WIN, LINE, D)), ANY],
        out_specs=(
            whole((GH, GW, D)),
            whole((WINDOWS * WIN, LINE, D)),
            pl.BlockSpec((D // 2, CHUNK), lambda i: (0, i)),
            pl.BlockSpec((D // 2, CHUNK), lambda i: (0, i)),
            pl.BlockSpec((D // 2, CHUNK), lambda i: (0, at(i))),
            pl.BlockSpec((D // 2, CHUNK), lambda i: (0, at(i))),
            whole((8, D)),
            whole((8, D)),
        ),
        scratch_shapes=[
            pltpu.VMEM((DENSE, D), f32),
            pltpu.VMEM((DENSE, D), bf16),
            pltpu.VMEM((DENSE, D), f32),
            pltpu.VMEM((DENSE, D), f32),
            pltpu.VMEM((DENSE, CHUNK), bf16),
            pltpu.VMEM((DENSE, CHUNK), bf16),
            pltpu.VMEM((DENSE, D), f32),
            pltpu.VMEM((DENSE, D), bf16),
            pltpu.VMEM((WINDOWS * TOK, D), bf16),
            pltpu.SemaphoreType.DMA((3,)),
        ],
        compiler_params=params(1),
        cost_estimate=pl.CostEstimate(flops=50_000_000_000, bytes_accessed=36_000_000, transcendentals=6_000_000),
        name="feed",
    )(core, images, cot, gupd, vec, weights, weights, branch, attended)


def backward(start, count, packed, soft, att, gbr, two, table, hot, before=()):
    per = lambda *shape: pl.BlockSpec(shape, lambda i: (start + i,) + (0,) * (len(shape) - 1))
    return pl.pallas_call(
        backward_kernel,
        grid=(count,),
        out_shape=(
            shaped((count * TOK, 3 * D), bf16),
            shaped((8, D), f32),
            shaped((256, 128), f32),
            flag_shape,
        ),
        in_specs=[
            per(TOK, 3 * D),
            per(HEADS, TOK, TOK),
            per(TOK, D),
            per(TOK, D),
            whole((D, 2 * D)),
            whole((128, 256)),
            whole((2, TOK, 128)),
        ]
        + [ANY] * len(before),
        out_specs=(pl.BlockSpec((TOK, 3 * D), lambda i: (i, 0)), whole((8, D)), whole((256, 128)), FLAG),
        scratch_shapes=[pltpu.VMEM((TOK, D), bf16)],
        compiler_params=params(1),
        cost_estimate=pl.CostEstimate(flops=6_000_000_000 * count, bytes_accessed=9_000_000, transcendentals=0),
        name="attend_back",
    )(packed, soft, att, gbr, two, table, hot, *before)


def attention_weights(core, sums, tiles, gpacked, gbias, before=()):
    return pl.pallas_call(
        attention_weights_kernel,
        grid=(1,),
        out_shape=(shaped((D // 2, 3 * D + 256), bf16),) * 2 + (flag_shape,),
        in_specs=[SMEM]
        + [whole((8, D))] * 3
        + [whole((WINDOWS * TOK, D))]
        + [ANY] * len(CALLS)
        + [whole((8, D))] * len(CALLS)
        + [ANY] * len(before),
        out_specs=(whole((D // 2, 3 * D + 256)),) * 2 + (FLAG,),
        scratch_shapes=[pltpu.VMEM((WINDOWS * TOK, 3 * D), bf16), pltpu.SemaphoreType.DMA((3 * len(CALLS),))],
        compiler_params=params(1),
        cost_estimate=pl.CostEstimate(flops=25_000_000_000, bytes_accessed=18_000_000, transcendentals=0),
        name="attend_weights",
    )(core, *sums, tiles, *gpacked, *gbias, *before)


def end(images, gbr, one, two, vec, gpacked, gtab, before=()):
    return pl.pallas_call(
        end_kernel,
        out_shape=(shaped((GH, GW, D), bf16), shaped((8, D), f32), shaped((64, 128), f32), flag_shape),
        in_specs=[ANY] * 2 + [VMEM] * 3 + [ANY] * len(CALLS) + [VMEM] * len(CALLS) + [ANY] * len(before),
        out_specs=(VMEM, VMEM, VMEM, FLAG),
        scratch_shapes=[
            pltpu.VMEM((WINDOWS * WIN, LINE, D), f32),
            pltpu.VMEM((WINDOWS * TOK, 3 * D), bf16),
            pltpu.VMEM((GH, GW, D), bf16),
            pltpu.VMEM((WINDOWS * WIN, LINE, D), bf16),
            pltpu.SemaphoreType.DMA((len(CALLS) + 2,)),
        ],
        compiler_params=params(),
        cost_estimate=pl.CostEstimate(flops=12_000_000_000, bytes_accessed=17_000_000, transcendentals=0),
        name="end",
    )(images, gbr, one, two, vec, *gpacked, *gtab, *before)


def pack(eight, up_bias, weight):
    return pl.pallas_call(
        pack_kernel,
        out_shape=shaped((weight.shape[0], 128 + 2 * D), bf16),
        in_specs=[VMEM] * 3,
        out_specs=VMEM,
        compiler_params=params(),
        name="pack",
    )(eight, up_bias, weight)


def one_hot_keys(flip):
    token = np.arange(TOK)
    row, col = token // LINE, token % LINE
    lane = np.arange(128)
    group, local = lane // 32, lane % 32
    hot = []
    for head in range(2):
        mine = (group % 2 == head)[None, :]
        value = ((local[None, :] == row[:, None]) & (local < WIN)[None, :]) | (
            (local[None, :] - 16 == (13 - col if flip else col)[:, None]) & (col < WIN)[:, None]
        )
        value = np.where(mine & value, 1.0, 0.0)
        value[:, 14] = np.where(col >= WIN, -1e30, 0.0)
        hot.append(value)
    return jnp.asarray(np.stack(hot), dtype=bf16)


AXES = ("dp", "fsdp")


class Exchange:
    def __init__(self, dp, fsdp):
        self.count = dp * fsdp
        self.bits = []
        bit = self.count // 2
        while bit:
            self.bits.append(bit)
            bit //= 2
        place = lax.axis_index(AXES).astype(jnp.int32)
        self.place = place
        self.mine = [(place >> (bit.bit_length() - 1)) & 1 for bit in self.bits]
        self.places = jnp.stack(self.mine)
        last = len(self.bits) - 1
        low = list(range(last - 1, 1, -1))
        self.orders = ([0, last] + low, [last, 0] + low)

    def swap(self, value, at):
        bit = self.bits[at]
        return lax.ppermute(value, AXES, [(i, i ^ bit) for i in range(self.count)])

    def spread(self, value):
        return value.reshape((1,) * len(self.bits) + value.shape)

    def join(self, value, at, flag=None):
        other = self.swap(value, at)
        mine = self.mine[at] if flag is None else self.mine[at] + flag[0]
        return jnp.where(
            mine == 0, jnp.concatenate([value, other], axis=at), jnp.concatenate([other, value], axis=at)
        )

    def own_part(self, piece, flag=None):
        terms, done, half = piece
        total = None
        for term in terms:
            for at in done:
                if term.shape[at] == 2:
                    mine = self.mine[at] if flag is None else self.mine[at] + flag[0]
                    term = lax.dynamic_index_in_dim(term, mine, at, keepdims=True)
            if half is not None:
                columns = term.shape[-1] // 2
                term = term[..., half * columns : (half + 1) * columns]
            term = term.astype(f32)
            total = term if total is None else total + term
        return total

    def halve(self, value, at):
        leave = lax.dynamic_index_in_dim(value, 1 - self.mine[at], at, keepdims=True).astype(bf16)
        stay = lax.dynamic_index_in_dim(value, self.mine[at], at, keepdims=True)
        return stay, self.swap(leave, at), leave

    def tie(self, values, before):
        count = len(values)

        def kernel(*refs):
            pass

        return pl.pallas_call(
            kernel,
            out_shape=tuple(shaped(v.shape, v.dtype) for v in values),
            in_specs=[ANY] * (count + len(before)),
            out_specs=(ANY,) * count,
            input_output_aliases={i: i for i in range(count)},
            name="tie",
        )(*values, *before)

    def flat(self, value):
        return value.reshape((self.count * value.shape[-2], value.shape[-1]))

    def cut(self, keep, send):
        rows, columns = keep.shape
        shape = (2, 1) + (2,) * (len(self.bits) - 2) + (2 * rows // self.count, columns)
        return [keep.reshape(shape), self.swap(send, 1).reshape(shape)]

    def blocks(self, piece, width, steps, leave=None):
        terms, done, half = piece
        specs = []
        for term in terms:
            shape = term.shape
            block, pick = [], []
            for at in range(len(self.bits)):
                cut = at in done or at == leave
                block.append(1 if cut else shape[at])
                pick.append((at, shape[at] == 2 and cut, at == leave))
            block += [shape[-2], width]
            first = half * steps if half and shape[-1] > width * steps else 0

            def index(i, places, pick=pick, first=first):
                where = [jnp.where(other, 1 - places[at], places[at]) if use else 0 for at, use, other in pick]
                return (*where, 0, first + jnp.minimum(i, steps - 1))

            specs.append(pl.BlockSpec(tuple(block), index))
        return specs

    def narrow(self, pieces, ats, widths, before=()):
        operands, specs, outs, out_specs, counts = [], [], [], [], []
        grid = 1
        for piece, at, width in zip(pieces, ats, widths):
            terms, done, half = piece
            columns = terms[-1].shape[-1] // (2 if half is not None and len(terms) == 2 else 1)
            steps = columns // width
            grid = max(grid, steps)
            specs += self.blocks(piece, width, steps, at)
            operands += terms
            counts.append(len(terms))
            shape = tuple(1 if i in done or i == at else n for i, n in enumerate(terms[0].shape[:-1]))
            outs.append(shaped(shape + (columns,), bf16))
            out_specs.append(
                pl.BlockSpec(
                    shape + (width,),
                    lambda i, places, n=len(shape), steps=steps: (0,) * n + (jnp.minimum(i, steps - 1),),
                )
            )
        count = len(pieces)

        def kernel(places, *refs):
            results = refs[-count - 1 : -1]
            refs[-1][0] = 0
            at = 0
            for i, terms in enumerate(counts):
                total = refs[at][...].astype(f32)
                for ref in refs[at + 1 : at + terms]:
                    total += ref[...].astype(f32)
                results[i][...] = total.astype(bf16)
                at += terms

        size = sum(int(np.prod(o.shape)) for o in outs)
        got = pl.pallas_call(
            kernel,
            grid_spec=pltpu.PrefetchScalarGridSpec(
                num_scalar_prefetch=1,
                grid=(grid,),
                in_specs=specs + [ANY] * len(before),
                out_specs=tuple(out_specs) + (FLAG,),
            ),
            out_shape=tuple(outs) + (flag_shape,),
            compiler_params=params(1),
            cost_estimate=pl.CostEstimate(flops=4 * size, bytes_accessed=8 * size, transcendentals=0),
            name="narrow",
        )(self.places, *operands, *before)
        results = []
        for (terms, done, half), at, leave in zip(pieces, ats, got):
            results.append((terms + [self.swap(leave, at)], done + [at], half))
        return results, [got[-1]]

    def close(self, pieces, kernel, out_shape, name, more=()):
        operands = [part.reshape(part.shape[-2:]) for piece in pieces for part in piece]

        def body(*refs):
            sums = [refs[2 * i][...] + refs[2 * i + 1][...].astype(f32) for i in range(len(pieces))]
            kernel(*sums, *refs[2 * len(pieces) :])

        return pl.pallas_call(
            body,
            out_shape=out_shape,
            in_specs=[VMEM] * (len(operands) + len(more)),
            out_specs=(VMEM,) * len(out_shape),
            compiler_params=params(),
            name=name,
        )(*operands, *more)


def local(
    dp,
    fsdp,
    images,
    grad_out,
    box_rows,
    box_cols,
    box_valid,
    box_count,
    in_weight,
    query_bias,
    value_bias,
    out_weight,
    out_bias,
    first_gain,
    first_shift,
    second_gain,
    second_shift,
    up_weight,
    up_bias,
    down_weight,
    down_bias,
    row_table,
    col_table,
):
    links = Exchange(dp, fsdp)
    image = images[0]
    core = (lax.axis_index("dp") & 1).astype(jnp.int32).reshape(1)
    hot = one_hot_keys(False)
    hot_back = one_hot_keys(True)
    eight = jnp.stack(
        [query_bias, value_bias, out_bias, first_gain, first_shift, second_gain, second_shift, down_bias]
    )
    first, second = links.orders[0][::-1], links.orders[1][::-1]
    last = len(first)
    two = links.spread(jnp.concatenate([in_weight[:, 2 * D :], out_weight], axis=1))
    one = links.spread(pack(eight, up_bias[None], in_weight))
    feed_weights = lax.all_gather(pack_feed(up_weight, down_weight), AXES, axis=0, tiled=True)
    for step in range(last - 2):
        two = links.join(two, second[step])
        one = links.join(one, first[step])
    cot, gupd, table, table_back, flag = weigh(
        box_count, grad_out[0], box_rows[0], box_cols[0], box_valid.reshape(NBOX, 1), row_table, col_table, [two, one]
    )
    two = links.join(two, second[last - 2], flag)
    one = links.join(one, first[last - 2], flag)
    unit, flag = begin(image, [two, one])
    unit = unit.reshape(WINDOWS * TOK, D)
    two = links.join(two, second[last - 1], flag)
    one = links.join(one, first[last - 1], flag)
    halves = [h.reshape(2, D // 4, -1) for h in (one, two, links.swap(one, 1), links.swap(two, 1))]

    tiles, packed, soft, att, branch, vec, one, two = forward(links.places, halves, unit, table, hot)
    block_out, gbr, gup_k, gup_s, gdown_k, gdown_s, gupb, sums2 = middle(
        core, image, cot, gupd, vec, feed_weights, branch.reshape(WINDOWS * WIN, LINE, D), att
    )

    first, second = links.orders
    gbr_flat = gbr.reshape(WINDOWS * TOK, D)
    feed = [(links.cut(gup_k, gup_s), [], None), (links.cut(gdown_k, gdown_s), [], None)]
    back = []
    flag = []
    start = 0
    for windows in CALLS:
        back.append(backward(start, windows, packed, soft, att, gbr_flat, two, table_back, hot_back, flag))
        flag = [back[-1][3]]
        if start == 0:
            feed, flag = links.narrow(feed, (first[0], second[0]), ((FF + D) // 2, FF // 2), flag)
        start += windows
    gpacked = [b[0] for b in back]
    image_grad, sums1, tables, flag = end(image, gbr, one, two, vec, gpacked, [b[2] for b in back], flag)
    feed, flag = links.narrow(feed, (first[1], second[1]), (FF + D, FF), [flag])
    all_tables = lax.all_gather(tables, AXES, axis=0, tiled=False)
    gin_k, gin_s, flag = attention_weights(core, (sums1, sums2, gupb), tiles, gpacked, [b[1] for b in back], flag)
    *recv, gin_s = links.tie([f[0][-1] for f in feed] + [gin_s], [flag])
    feed = [(f[0][:-1] + [r], f[1], f[2]) for f, r in zip(feed, recv)]
    gin = links.cut(gin_k, gin_s)
    feed = [links.halve(links.own_part(f), at) for f, at in zip(feed, (first[2], second[2]))]
    gin = [(links.own_part((gin, [], half)),) for half in range(2)]
    for step in range(last):
        gin = [links.halve(sum(g), at) for g, at in zip([(g[0],) if len(g) == 1 else g[:2] for g in gin], (first[step], second[step]))]
        if 1 <= step < last - 2 or step == last - 1:
            late = links.tie([f[1] for f in feed], [g[2] for g in gin])
            feed = [(f[0], r) for f, r in zip(feed, late)]
        if 1 <= step < last - 2:
            ats = (first[step + 2], second[step + 2])
            feed = [links.halve(f[0] + f[1].astype(f32), at) for f, at in zip(feed, ats)]
    gin = [g[:2] for g in gin]
    feed = [f[:2] for f in feed]
    own = in_weight.shape[0]
    gup, gout, gdown = links.close(
        feed, unpack_feed_kernel, (shaped((own, FF), f32), shaped((own, D), f32), shaped((4 * own, D), f32)), "unpack_feed"
    )
    entries = 2 * WIN - 1
    gin, *out = links.close(
        gin,
        unpack_in_kernel,
        (shaped((own, 3 * D), f32),)
        + (shaped((1, own), f32),) * 8
        + (shaped((1, 4 * own), f32),)
        + (shaped((entries, HD), f32),) * 2,
        "unpack_in",
        [all_tables],
    )
    qb, vb, ob, g1, s1, g2, s2, db, ub = [o.reshape(-1) for o in out[:9]]
    row_grad, col_grad = out[9:]
    return (
        block_out[None],
        image_grad[None],
        gin,
        qb,
        vb,
        gout,
        ob,
        g1,
        s1,
        g2,
        s2,
        gup,
        ub,
        gdown,
        db,
        row_grad,
        col_grad,
    )


def solution(mesh):
    rows = P(AXES)
    dp, fsdp = mesh.shape["dp"], mesh.shape["fsdp"]
    return jax.shard_map(
        lambda *args: local(dp, fsdp, *args),
        mesh=mesh,
        in_specs=(rows,) * 19 + (P(), P()),
        out_specs=(rows,) * 15 + (P(), P()),
        check_vma=False,
    )
```

profile of v0, /device:TPU:0, one launch (start us, length us, event | category | flops | bytes accessed | tf_op | source)
XLA Modules:
  0.0 321.0 jit_solution(7963630726531006611)
XLA Ops:
  7.3 2.0 pack_feed.1
  9.3 0.8 slice.15
  10.1 0.8 fusion.12
  10.9 4.1 %collective-permute-start = (bf16[1,1,1,1,1,24,1536]{6,5,4,3,2,1,0:T(8,128)(2,1)S(1)}, bf16[1,1,1,1,1,24,1536]{6,5,4,3,2,1,0:T(8,128)(2,1)S(1)}, u32[]{:S(2)}, u32[]{:S(2)}) collective-permute-start(bf16[1,1,1,1,1,24,1536]{6,5,4,3,2,1,0:T(8,128)(2,1)S(1)} %get-tuple-element.165), channel_id=1, source_target_pairs={{0,4},{1,5},{2,6},{3,7},{4,0},{5,1},{6,2},{7,3},{8,12},{9,13},{10,... | collective-permute-start | bytes 221192 | tf_op jit(solution)/shard_map/ppermute | solution.py:813
  15.0 1.4 stack.53.eight_ref
  16.3 1.7 pack.1
  18.1 1.5 copy.62
  19.6 0.8 copy.63
  20.4 0.8 copy.68.valid_ref
  21.9 1.9 collective-permute-start.1
  23.8 1.1 collective-permute-done.2
  25.0 1.0 fusion.7
  26.4 4.9 %collective-permute-done.1 = bf16[1,1,2,1,1,24,1536]{6,5,2,4,3,1,0:T(8,128)(2,1)S(1)} collective-permute-done((bf16[1,1,2,1,1,24,1536]{6,5,2,4,3,1,0:T(8,128)(2,1)S(1)}, bf16[1,1,2,1,1,24,1536]{6,5,2,4,3,1,0:T(8,128)(2,1)S(1)}, u32[]{:S(2)}, u32[]{:S(2)}) %collective-permute-start.1) | collective-permute-done | bytes 147488 | tf_op jit(solution)/shard_map/ppermute | solution.py:813
  32.8 1.8 collective-permute-start.4
  34.6 1.8 collective-permute-done.3
  36.5 1.6 collective-permute-start.5
  39.0 4.9 %weigh.1 = (f32[992,768]{1,0:T(8,128)}, bf16[992,768]{1,0:T(8,128)(2,1)}, bf16[128,256]{1,0:T(8,128)(2,1)}, bf16[128,256]{1,0:T(8,128)(2,1)}, s32[1]{0:T(128)}) custom-call(s32[1]{0:T(128)S(6)} %copy.90.count_ref, bf16[26,38,768]{2,1,0:T(8,128)(2,1)} %bitcast.127, s32[300,2]{1,0:T(8,128)} %bitcast.139, s32[300,2]{1,0:T(8,128)} %bitcast.140, ...), custom_call_target="tpu_custom_call" | custom-call | flops 30000000 | bytes 6000000 | tf_op jit(solution)/shard_map/weigh/pallas_call | solution.py:593
  45.2 0.8 maximum_select_fusion.5
  46.2 1.6 collective-permute-start.6
  48.0 1.4 collective-permute-start.7
  49.4 1.2 fusion.6
  50.6 4.9 %begin.1 = (f32[84,16,768]{2,1,0:T(8,128)}, s32[1]{0:T(128)}) custom-call(bf16[26,38,768]{2,1,0:T(8,128)(2,1)} %bitcast.128, bf16[2,1,2,2,1,24,1536]{6,5,4,3,2,1,0:T(8,128)(2,1)} %copy-done.1, bf16[1,1,2,2,2,24,1664]{6,5,4,3,2,1,0:T(8,128)(2,1)} %copy-done.13), custom_call_target="tpu_custom_call" | custom-call | flops 30000000 | bytes 6000000 | tf_op jit(solution)/shard_map/begin/pallas_call | solution.py:581
  56.8 1.3 fusion.4
  58.1 5.3 %collective-permute-done.6 = bf16[1,1,2,2,2,24,1664]{6,5,4,3,2,1,0:T(8,128)(2,1)S(1)} collective-permute-done((bf16[1,1,2,2,2,24,1664]{6,5,4,3,2,1,0:T(8,128)(2,1)S(1)}, bf16[1,1,2,2,2,24,1664]{6,5,4,3,2,1,0:T(8,128)(2,1)S(1)}, u32[]{:S(2)}, u32[]{:S(2)}) %collective-permute-start.6) | collective-permute-done | bytes 639008 | tf_op jit(solution)/shard_map/ppermute | solution.py:813
  63.4 1.4 maximum_select_fusion.1
  64.8 1.9 collective-permute-done.7
  66.7 3.0 fusion.1
  70.2 1.3 maximum_select_fusion.refs_0_
  71.5 1.2 collective-permute-done.9
  72.7 1.1 copy-done.29
  73.8 31.6 %attend.1 = (bf16[1344,768]{1,0:T(8,128)(2,1)}, bf16[1344,2304]{1,0:T(8,128)(2,1)}, bf16[72,224,224]{2,1,0:T(8,128)(2,1)}, bf16[1344,768]{1,0:T(8,128)(2,1)}, f3...) custom-call(s32[5]{0:T(128)} %stack.59.places_ref.places, ...), custom_call_target="tpu_custom_call" | custom-call | flops 30000001024 | bytes 28000000 | tf_op jit(solution)/shard_map/attend/pallas_call | solution.py:612
  105.4 68.1 %feed.1 = (bf16[26,38,768]{2,1,0:T(8,128)(2,1)}, bf16[84,16,768]{2,1,0:T(8,128)(2,1)}, bf16[384,3840]{1,0:T(8,128)(2,1)}, bf16[384,3840]{1,0:T(8,128)(2,1)}, bf1...) custom-call(s32[1]{0:T(128)} %bitcast.core_ref, ...), custom_call_target="tpu_custom_call" | custom-call | flops 49999998976 | bytes 36000000 | tf_op jit(solution)/shard_map/feed/pallas_call | solution.py:646
  174.1 11.8 %attend_back.2 = (bf16[448,2304]{1,0:T(8,128)(2,1)}, f32[8,768]{1,0:T(8,128)}, f32[256,128]{1,0:T(8,128)}, s32[1]{0:T(128)}) custom-call(bf16[1344,2304]{1,0:T(8,128)(2,1)} %get-tuple-element.96.packed_ref, bf16[72,224,224]{2,1,0:T(8,128)(2,1)} %get-tuple-element.97.soft_ref, bf16[1344,768]{1,0:T(8,128)(2,1)} %get-tuple-element.91.refs_1_.att_ref, ...), custom_call_target="tpu_custom_call" | custom-call | flops 12000000000 | bytes 9000000 | tf_op jit(solution)/shard_map/attend_back/pallas_call | solution.py:699
  185.9 1.7 copy-done
  187.6 5.2 %narrow.2 = (bf16[1,1,2,2,2,24,3840]{6,5,4,3,2,1,0:T(8,128)(2,1)}, bf16[2,1,2,2,1,24,3072]{6,5,4,3,2,1,0:T(8,128)(2,1)}, s32[1]{0:T(128)}) custom-call(s32[5]{0:T(128)} %stack.59.places_ref.places, bf16[2,1,2,2,2,24,3840]{6,5,4,3,2,1,0:T(8,128)(2,1)} %bitcast.110, bf16[2,1,2,2,2,24,3840]{6,5,4,3,2,1,0:T(8,128)(2,1)} %bitcast.113, ...), custom_call_target="tpu_custom_call" | custom-call | flops 5308416 | bytes 10616832 | tf_op jit(solution)/shard_map/narrow/pallas_call | solution.py:921
  192.8 1.5 collective-permute-start.12
  194.3 1.1 collective-permute-start.13
  195.3 20.1 %attend_back.3 = (bf16[896,2304]{1,0:T(8,128)(2,1)}, f32[8,768]{1,0:T(8,128)}, f32[256,128]{1,0:T(8,128)}, s32[1]{0:T(128)}) custom-call(bf16[1344,2304]{1,0:T(8,128)(2,1)} %get-tuple-element.96.packed_ref, bf16[72,224,224]{2,1,0:T(8,128)(2,1)} %get-tuple-element.97.soft_ref, bf16[1344,768]{1,0:T(8,128)(2,1)} %get-tuple-element.91.refs_1_.att_ref, ...), custom_call_target="tpu_custom_call" | custom-call | flops 24000000000 | bytes 9000000 | tf_op jit(solution)/shard_map/attend_back/pallas_call | solution.py:699
  215.4 16.1 %end.1 = (bf16[26,38,768]{2,1,0:T(8,128)(2,1)}, f32[8,768]{1,0:T(8,128)}, f32[64,128]{1,0:T(8,128)}, s32[1]{0:T(128)}) custom-call(bf16[26,38,768]{2,1,0:T(8,128)(2,1)} %bitcast.130, bf16[84,16,768]{2,1,0:T(8,128)(2,1)} %get-tuple-element.93.gbr_ref, bf16[768,1664]{1,0:T(8,128)(2,1)} %get-tuple-element.94.one_ref, ...), custom_call_target="tpu_custom_call" | custom-call | flops 12000000000 | bytes 17000000 | tf_op jit(solution)/shard_map/end/pallas_call | solution.py:746
  231.6 1.0 copy-done.11
  233.1 4.8 %narrow.3 = (bf16[1,1,2,2,1,24,3840]{6,5,4,3,2,1,0:T(8,128)(2,1)}, bf16[1,1,2,2,1,24,3072]{6,5,4,3,2,1,0:T(8,128)(2,1)}, s32[1]{0:T(128)}) custom-call(s32[5]{0:T(128)} %stack.59.places_ref.places, bf16[2,1,2,2,2,24,3840]{6,5,4,3,2,1,0:T(8,128)(2,1)} %bitcast.111, bf16[2,1,2,2,2,24,3840]{6,5,4,3,2,1,0:T(8,128)(2,1)} %bitcast.114, ...), custom_call_target="tpu_custom_call" | custom-call | flops 2654208 | bytes 5308416 | tf_op jit(solution)/shard_map/narrow/pallas_call | solution.py:921
  237.9 1.0 collective-permute-start.14
  239.5 13.6 %attend_weights.1 = (bf16[384,2560]{1,0:T(8,128)(2,1)}, bf16[384,2560]{1,0:T(8,128)(2,1)}, s32[1]{0:T(128)}) custom-call(s32[1]{0:T(128)} %bitcast.core_ref, f32[8,768]{1,0:T(8,128)} %get-tuple-element.111.sums1_ref, f32[8,768]{1,0:T(8,128)} %get-tuple-element.112.sums2_ref, f32[8,768]{1,0:T(8,128)} %get-tuple-element.113.gupb_ref, ...), custom_call_target="tpu_custom_call" | custom-call | flops 24999999488 | bytes 18000000 | tf_op jit(solution)/shard_map/attend_weights/pallas_call | solution.py:727
  253.0 1.1 collective-permute-done.15.refs_1_
  254.1 2.3 collective-permute-done.14.refs_0_
  256.4 0.9 copy-done.9
  258.6 1.9 convert_add_fusion.3
  260.5 2.6 collective-permute-start.26
  263.2 1.8 convert_add_fusion.2
  267.1 13.6 %collective-permute-done.21 = bf16[2,1,2,2,1,24,1280]{6,5,4,3,2,1,0:T(8,128)(2,1)S(1)} collective-permute-done((bf16[2,1,2,2,1,24,1280]{6,5,4,3,2,1,0:T(8,128)(2,1)S(1)}, bf16[2,1,2,2,1,24,1280]{6,5,4,3,2,1,0:T(8,128)(2,1)S(1)}, u32[]{:S(2)}, u32[]{:S(2)}) %collective-permute-start.21) | collective-permute-done | bytes 491552 | tf_op jit(solution)/shard_map/ppermute | solution.py:813
  281.8 0.9 copy-done.7
  282.7 0.9 collective-permute-start.18
  284.4 1.1 convert_add_fusion.7
  285.5 2.8 collective-permute-start.28
  288.7 0.8 dynamic-slice_bitcast_fusion.refs_0_
  290.2 1.0 convert_add_fusion.8
  291.2 2.7 collective-permute-start.23
  293.9 1.0 convert_add_fusion.9
  295.1 5.5 %collective-permute-done.23 = bf16[1,1,2,1,1,24,1280]{6,5,4,3,2,1,0:T(8,128)(2,1)S(1)} collective-permute-done((bf16[1,1,2,1,1,24,1280]{6,5,4,3,2,1,0:T(8,128)(2,1)S(1)}, bf16[1,1,2,1,1,24,1280]{6,5,4,3,2,1,0:T(8,128)(2,1)S(1)}, u32[]{:S(2)}, u32[]{:S(2)}) %collective-permute-start.23) | collective-permute-done | bytes 122912 | tf_op jit(solution)/shard_map/ppermute | solution.py:813
  300.6 1.0 collective-permute-start.24
  301.6 2.2 collective-permute-done.19
  303.9 2.1 collective-permute-start.20
  308.6 2.5 unpack_feed.1
  311.8 2.2 unpack_in.1
  (133 shorter events, 15.4 us)
Async XLA Ops:
  7.2 12.4 %copy-start.27 = (s32[1,300,2]{1,2,0:T(2,128)S(1)}, s32[1,300,2]{1,2,0:T(2,128)}, u32[]{:S(2)}) copy-start(s32[1,300,2]{1,2,0:T(2,128)} %param.26) | copy-start | bytes 7204
  7.2 13.2 %copy-start.28 = (s32[1,300]{1,0:T(1,128)S(1)}, s32[1,300]{1,0:T(1,128)}, u32[]{:S(2)}) copy-start(s32[1,300]{1,0:T(1,128)} %param.27) | copy-start | bytes 3604
  7.2 98.2 %all-gather.4.cloned.1.call-start = ((), (), s32[]{:S(2)}) async-start(), calls=%async_computation | async-start | bytes 9732096 | tf_op jit(solution)/shard_map/all_gather | solution.py:993
  9.2 301.9 %all-gather.6.cloned.1.call-start = ((), (), s32[]{:S(2)}) async-start(), calls=%async_computation.1 | async-start | bytes 1081344 | tf_op jit(solution)/shard_map/all_gather | solution.py:1028
  10.9 11.0 %collective-permute-start = (bf16[1,1,1,1,1,24,1536]{6,5,4,3,2,1,0:T(8,128)(2,1)S(1)}, bf16[1,1,1,1,1,24,1536]{6,5,4,3,2,1,0:T(8,128)(2,1)S(1)}, u32[]{:S(2)}, u32[]{:S(2)}) collective-permute-start(bf16[1,1,1,1,1,24,1536]{6,5,4,3,2,1,0:T(8,128)(2,1)S(1)} %get-tuple-element.165), channel_id=1, source_target_pairs={{0,4},{1,5},{2,6},{3,7},{4,0},{5,1},{6,2},{7,3},{8,12},{9,13},{10,... | collective-permute-start | bytes 221192 | tf_op jit(solution)/shard_map/ppermute | solution.py:813
  18.0 8.3 %copy-start.21 = (bf16[24,1664]{1,0:T(8,128)(2,1)S(1)}, bf16[24,1664]{1,0:T(8,128)(2,1)}, u32[]{:S(2)}) copy-start(bf16[24,1664]{1,0:T(8,128)(2,1)} %pack.1) | copy-start | bytes 239620
  18.0 6.9 %collective-permute-start.2 = (bf16[1,1,1,1,1,24,1664]{6,5,4,3,2,1,0:T(8,128)(2,1)}, bf16[1,1,1,1,1,24,1664]{6,5,4,3,2,1,0:T(8,128)(2,1)S(1)}, u32[]{:S(2)}, u32[]{:S(2)}) collective-permute-start(bf16[1,1,1,1,1,24,1664]{6,5,4,3,2,1,0:T(8,128)(2,1)} %bitcast.136), channel_id=1, source_target_pairs={{0,4},{1,5},{2,6},{3,7},{4,0},{5,1},{6,2},{7,3},{8,12},{9,13},{10,... | collective-permute-start | bytes 239624 | tf_op jit(solution)/shard_map/ppermute | solution.py:813
  21.9 9.4 %collective-permute-start.1 = (bf16[1,1,2,1,1,24,1536]{6,5,2,4,3,1,0:T(8,128)(2,1)S(1)}, bf16[1,1,2,1,1,24,1536]{6,5,2,4,3,1,0:T(8,128)(2,1)S(1)}, u32[]{:S(2)}, u32[]{:S(2)}) collective-permute-start(bf16[1,1,2,1,1,24,1536]{6,5,2,4,3,1,0:T(8,128)(2,1)S(1)} %fusion.8), channel_id=1, source_target_pairs={{0,2},{1,3},{2,0},{3,1},{4,6},{5,7},{6,4},{7,5},{8,10},{9,11},{10,... | collective-permute-start | bytes 442376 | tf_op jit(solution)/shard_map/ppermute | solution.py:813
  26.0 10.5 %collective-permute-start.3 = (bf16[1,1,2,1,1,24,1664]{6,5,2,4,3,1,0:T(8,128)(2,1)S(1)}, bf16[1,1,2,1,1,24,1664]{6,5,2,4,3,1,0:T(8,128)(2,1)S(1)}, u32[]{:S(2)}, u32[]{:S(2)}) collective-permute-start(bf16[1,1,2,1,1,24,1664]{6,5,2,4,3,1,0:T(8,128)(2,1)S(1)} %fusion.7), channel_id=1, source_target_pairs={{0,2},{1,3},{2,0},{3,1},{4,6},{5,7},{6,4},{7,5},{8,10},{9,11},{10,... | collective-permute-start | bytes 479240 | tf_op jit(solution)/shard_map/ppermute | solution.py:813
  32.8 15.0 %collective-permute-start.4 = (bf16[1,1,2,2,1,24,1536]{6,5,3,2,4,1,0:T(8,128)(2,1)}, bf16[1,1,2,2,1,24,1536]{6,5,3,2,4,1,0:T(8,128)(2,1)S(1)}, u32[]{:S(2)}, u32[]{:S(2)}) collective-permute-start(bf16[1,1,2,2,1,24,1536]{6,5,3,2,4,1,0:T(8,128)(2,1)} %copy.71), channel_id=1, source_target_pairs={{0,16},{1,17},{2,18},{3,19},{4,20},{5,21},{6,22},{7,23},{8,24},{9,... | collective-permute-start | bytes 884744 | tf_op jit(solution)/shard_map/ppermute | solution.py:813
  36.5 9.5 %collective-permute-start.5 = (bf16[1,1,2,2,1,24,1664]{6,5,2,3,4,1,0:T(8,128)(2,1)S(1)}, bf16[1,1,2,2,1,24,1664]{6,5,2,3,4,1,0:T(8,128)(2,1)S(1)}, u32[]{:S(2)}, u32[]{:S(2)}) collective-permute-start(bf16[1,1,2,2,1,24,1664]{6,5,2,3,4,1,0:T(8,128)(2,1)S(1)} %maximum_select_fusion.3), channel_id=1, source_target_pairs={{0,1},{1,0},{2,3},{3,2},{4,5},{5,4},{6,7},{7,6},{8,9},{9,8},{10,11... | collective-permute-start | bytes 958472 | tf_op jit(solution)/shard_map/ppermute | solution.py:813
  46.2 4.3 %copy-start.13 = (bf16[1,1,2,2,2,24,1664]{6,5,4,3,2,1,0:T(8,128)(2,1)}, bf16[1,1,2,2,2,24,1664]{6,5,4,3,2,1,0:T(8,128)(2,1)S(1)}, u32[]{:S(2)}) copy-start(bf16[1,1,2,2,2,24,1664]{6,5,4,3,2,1,0:T(8,128)(2,1)S(1)} %copy_select_fusion.refs_1_) | copy-start | bytes 1916932
  46.2 17.2 %collective-permute-start.6 = (bf16[1,1,2,2,2,24,1664]{6,5,4,3,2,1,0:T(8,128)(2,1)S(1)}, bf16[1,1,2,2,2,24,1664]{6,5,4,3,2,1,0:T(8,128)(2,1)S(1)}, u32[]{:S(2)}, u32[]{:S(2)}) collective-permute-start(bf16[1,1,2,2,2,24,1664]{6,5,4,3,2,1,0:T(8,128)(2,1)S(1)} %copy_select_fusion.refs_1_), channel_id=1, source_target_pairs={{0,16},{1,17},{2,18},{3,19},{4,20},{5,21},{6,22},{7,23},{8,24},{9,... | collective-permute-start | bytes 1916936 | tf_op jit(solution)/shard_map/ppermute | solution.py:813
  47.9 1.5 copy-start.17
  48.0 2.6 copy-start.1
  48.0 18.7 %collective-permute-start.7 = (bf16[2,1,2,2,1,24,1536]{6,5,4,3,2,1,0:T(8,128)(2,1)S(1)}, bf16[2,1,2,2,1,24,1536]{6,5,4,3,2,1,0:T(8,128)(2,1)}, u32[]{:S(2)}, u32[]{:S(2)}) collective-permute-start(bf16[2,1,2,2,1,24,1536]{6,5,4,3,2,1,0:T(8,128)(2,1)S(1)} %fusion.5.refs_0_), channel_id=1, source_target_pairs={{0,1},{1,0},{2,3},{3,2},{4,5},{5,4},{6,7},{7,6},{8,9},{9,8},{10,11... | collective-permute-start | bytes 1769480 | tf_op jit(solution)/shard_map/ppermute | solution.py:813
  58.1 8.6 %copy-start.2 = (bf16[2,1,2,2,1,24,1536]{6,5,4,3,2,1,0:T(8,128)(2,1)S(1)}, bf16[2,1,2,2,1,24,1536]{6,5,4,3,2,1,0:T(8,128)(2,1)}, u32[]{:S(2)}) copy-start(bf16[2,1,2,2,1,24,1536]{6,5,4,3,2,1,0:T(8,128)(2,1)} %copy-done.1) | copy-start | bytes 1769476
  64.8 7.9 %collective-permute-start.8 = (bf16[2,1,2,2,2,24,1664]{6,5,4,3,2,1,0:T(8,128)(2,1)}, bf16[2,1,2,2,2,24,1664]{6,5,4,3,2,1,0:T(8,128)(2,1)}, u32[]{:S(2)}, u32[]{:S(2)}) collective-permute-start(bf16[2,1,2,2,2,24,1664]{6,5,4,3,2,1,0:T(8,128)(2,1)} %maximum_select_fusion.1), channel_id=1, source_target_pairs={{0,8},{1,9},{2,10},{3,11},{4,12},{5,13},{6,14},{7,15},{8,0},{9,1},... | collective-permute-start | bytes 3833864 | tf_op jit(solution)/shard_map/ppermute | solution.py:813
  69.6 3.1 collective-permute-start.9
  72.7 1.1 copy-start.29
  173.6 12.4 %collective-permute-start.10 = (bf16[384,3840]{1,0:T(8,128)(2,1)}, bf16[384,3840]{1,0:T(8,128)(2,1)S(1)}, u32[]{:S(2)}, u32[]{:S(2)}) collective-permute-start(bf16[384,3840]{1,0:T(8,128)(2,1)} %get-tuple-element.101), channel_id=1, source_target_pairs={{0,8},{1,9},{2,10},{3,11},{4,12},{5,13},{6,14},{7,15},{8,0},{9,1},... | collective-permute-start | bytes 8847368 | tf_op jit(solution)/shard_map/ppermute | solution.py:813
  173.8 12.1 %collective-permute-start.11 = (bf16[384,3072]{1,0:T(8,128)(2,1)}, bf16[384,3072]{1,0:T(8,128)(2,1)}, u32[]{:S(2)}, u32[]{:S(2)}) collective-permute-start(bf16[384,3072]{1,0:T(8,128)(2,1)} %get-tuple-element.103), channel_id=1, source_target_pairs={{0,8},{1,9},{2,10},{3,11},{4,12},{5,13},{6,14},{7,15},{8,0},{9,1},... | collective-permute-start | bytes 7077896 | tf_op jit(solution)/shard_map/ppermute | solution.py:813
  185.9 1.7 copy-start
  192.8 38.8 %collective-permute-start.12 = (bf16[1,1,2,2,2,24,3840]{6,5,4,3,2,1,0:T(8,128)(2,1)}, bf16[1,1,2,2,2,24,3840]{6,5,4,3,2,1,0:T(8,128)(2,1)S(1)}, u32[]{:S(2)}, u32[]{:S(2)}) collective-permute-start(bf16[1,1,2,2,2,24,3840]{6,5,4,3,2,1,0:T(8,128)(2,1)} %get-tuple-element.117), channel_id=1, source_target_pairs={{0,16},{1,17},{2,18},{3,19},{4,20},{5,21},{6,22},{7,23},{8,24},{9,... | collective-permute-start | bytes 4423688 | tf_op jit(solution)/shard_map/ppermute | solution.py:813
  194.3 37.3 %collective-permute-start.13 = (bf16[2,1,2,2,1,24,3072]{6,5,4,3,2,1,0:T(8,128)(2,1)}, bf16[2,1,2,2,1,24,3072]{6,5,4,3,2,1,0:T(8,128)(2,1)S(1)}, u32[]{:S(2)}, u32[]{:S(2)}) collective-permute-start(bf16[2,1,2,2,1,24,3072]{6,5,4,3,2,1,0:T(8,128)(2,1)} %get-tuple-element.118), channel_id=1, source_target_pairs={{0,1},{1,0},{2,3},{3,2},{4,5},{5,4},{6,7},{7,6},{8,9},{9,8},{10,11... | collective-permute-start | bytes 3538952 | tf_op jit(solution)/shard_map/ppermute | solution.py:813
  231.6 1.0 copy-start.11
  231.6 1.5 copy-start.3
  237.9 18.6 %collective-permute-start.14 = (bf16[1,1,2,2,1,24,3840]{6,5,4,3,2,1,0:T(8,128)(2,1)}, bf16[1,1,2,2,1,24,3840]{6,5,4,3,2,1,0:T(8,128)(2,1)S(1)}, u32[]{:S(2)}, u32[]{:S(2)}) collective-permute-start(bf16[1,1,2,2,1,24,3840]{6,5,4,3,2,1,0:T(8,128)(2,1)} %get-tuple-element.122), channel_id=1, source_target_pairs={{0,1},{1,0},{2,3},{3,2},{4,5},{5,4},{6,7},{7,6},{8,9},{9,8},{10,11... | collective-permute-start | bytes 2211848 | tf_op jit(solution)/shard_map/ppermute | solution.py:813
  238.9 15.2 %collective-permute-start.15 = (bf16[1,1,2,2,1,24,3072]{6,5,4,3,2,1,0:T(8,128)(2,1)}, bf16[1,1,2,2,1,24,3072]{6,5,4,3,2,1,0:T(8,128)(2,1)}, u32[]{:S(2)}, u32[]{:S(2)}) collective-permute-start(bf16[1,1,2,2,1,24,3072]{6,5,4,3,2,1,0:T(8,128)(2,1)} %get-tuple-element.123), channel_id=1, source_target_pairs={{0,16},{1,17},{2,18},{3,19},{4,20},{5,21},{6,22},{7,23},{8,24},{9,... | collective-permute-start | bytes 1769480 | tf_op jit(solution)/shard_map/ppermute | solution.py:813
  256.4 0.9 copy-start.9
  257.3 1.3 copy-start.12
  258.1 7.0 %collective-permute-start.16 = (bf16[384,2560]{1,0:T(8,128)(2,1)}, bf16[384,2560]{1,0:T(8,128)(2,1)S(1)}, u32[]{:S(2)}, u32[]{:S(2)}) collective-permute-start(bf16[384,2560]{1,0:T(8,128)(2,1)} %get-tuple-element.126), channel_id=1, source_target_pairs={{0,8},{1,9},{2,10},{3,11},{4,12},{5,13},{6,14},{7,15},{8,0},{9,1},... | collective-permute-start | bytes 5898248 | tf_op jit(solution)/shard_map/ppermute | solution.py:813
  258.6 4.6 %copy-start.4 = (bf16[1,1,2,2,2,24,3840]{6,5,4,3,2,1,0:T(8,128)(2,1)S(1)}, bf16[1,1,2,2,2,24,3840]{6,5,4,3,2,1,0:T(8,128)(2,1)}, u32[]{:S(2)}) copy-start(bf16[1,1,2,2,2,24,3840]{6,5,4,3,2,1,0:T(8,128)(2,1)} %copy-done.3) | copy-start | bytes 4423684
  258.6 4.6 %copy-start.10 = (bf16[1,1,2,2,1,24,3840]{6,5,4,3,2,1,0:T(8,128)(2,1)S(1)}, bf16[1,1,2,2,1,24,3840]{6,5,4,3,2,1,0:T(8,128)(2,1)}, u32[]{:S(2)}) copy-start(bf16[1,1,2,2,1,24,3840]{6,5,4,3,2,1,0:T(8,128)(2,1)} %get-tuple-element.131) | copy-start | bytes 2211844
  260.5 23.2 %collective-permute-start.26 = (bf16[1,1,2,1,1,24,3072]{6,5,4,3,2,1,0:T(8,128)(2,1)S(1)}, bf16[1,1,2,1,1,24,3072]{6,5,4,3,2,1,0:T(8,128)(2,1)}, u32[]{:S(2)}, u32[]{:S(2)}) collective-permute-start(bf16[1,1,2,1,1,24,3072]{6,5,4,3,2,1,0:T(8,128)(2,1)S(1)} %dynamic-slice_convert_fusion.3), channel_id=1, source_target_pairs={{0,2},{1,3},{2,0},{3,1},{4,6},{5,7},{6,4},{7,5},{8,10},{9,11},{10,... | collective-permute-start | bytes 884744 | tf_op jit(solution)/shard_map/ppermute | solution.py:813
  263.2 2.0 copy-start.14
  265.8 14.9 %collective-permute-start.21 = (bf16[2,1,2,2,1,24,1280]{6,5,4,3,2,1,0:T(8,128)(2,1)S(1)}, bf16[2,1,2,2,1,24,1280]{6,5,4,3,2,1,0:T(8,128)(2,1)S(1)}, u32[]{:S(2)}, u32[]{:S(2)}) collective-permute-start(bf16[2,1,2,2,1,24,1280]{6,5,4,3,2,1,0:T(8,128)(2,1)S(1)} %dynamic-slice_convert_fusion), channel_id=1, source_target_pairs={{0,1},{1,0},{2,3},{3,2},{4,5},{5,4},{6,7},{7,6},{8,9},{9,8},{10,11... | collective-permute-start | bytes 1474568 | tf_op jit(solution)/shard_map/ppermute | solution.py:813
  266.5 17.2 %collective-permute-start.25 = (bf16[1,1,2,1,1,24,3840]{6,5,4,3,2,1,0:T(8,128)(2,1)S(1)}, bf16[1,1,2,1,1,24,3840]{6,5,4,3,2,1,0:T(8,128)(2,1)S(1)}, u32[]{:S(2)}, u32[]{:S(2)}) collective-permute-start(bf16[1,1,2,1,1,24,3840]{6,5,4,3,2,1,0:T(8,128)(2,1)S(1)} %dynamic-slice_convert_fusion.2), channel_id=1, source_target_pairs={{0,2},{1,3},{2,0},{3,1},{4,6},{5,7},{6,4},{7,5},{8,10},{9,11},{10,... | collective-permute-start | bytes 1105928 | tf_op jit(solution)/shard_map/ppermute | solution.py:813
  266.7 14.8 %collective-permute-start.17 = (bf16[1,1,2,2,2,24,1280]{6,5,4,3,2,1,0:T(8,128)(2,1)S(1)}, bf16[1,1,2,2,2,24,1280]{6,5,4,3,2,1,0:T(8,128)(2,1)S(1)}, u32[]{:S(2)}, u32[]{:S(2)}) collective-permute-start(bf16[1,1,2,2,2,24,1280]{6,5,4,3,2,1,0:T(8,128)(2,1)S(1)} %dynamic-slice_convert_fusion.1), channel_id=1, source_target_pairs={{0,16},{1,17},{2,18},{3,19},{4,20},{5,21},{6,22},{7,23},{8,24},{9,... | collective-permute-start | bytes 1474568 | tf_op jit(solution)/shard_map/ppermute | solution.py:813
  280.8 1.0 copy-start.5
  280.9 1.0 copy-start.18
  280.9 9.3 %collective-permute-start.22 = (bf16[1,1,2,2,1,24,1280]{6,5,4,3,2,1,0:T(8,128)(2,1)S(1)}, bf16[1,1,2,2,1,24,1280]{6,5,4,3,2,1,0:T(8,128)(2,1)}, u32[]{:S(2)}, u32[]{:S(2)}) collective-permute-start(bf16[1,1,2,2,1,24,1280]{6,5,4,3,2,1,0:T(8,128)(2,1)S(1)} %dynamic-slice_convert_fusion.4.refs_3_), channel_id=1, source_target_pairs={{0,16},{1,17},{2,18},{3,19},{4,20},{5,21},{6,22},{7,23},{8,24},{9,... | collective-permute-start | bytes 737288 | tf_op jit(solution)/shard_map/ppermute | solution.py:813
  281.8 1.0 copy-start.7
  282.7 1.0 copy-start.19
  282.7 11.2 %collective-permute-start.18 = (bf16[1,1,2,2,1,24,1280]{6,5,4,3,2,1,0:T(8,128)(2,1)S(1)}, bf16[1,1,2,2,1,24,1280]{6,5,4,3,2,1,0:T(8,128)(2,1)}, u32[]{:S(2)}, u32[]{:S(2)}) collective-permute-start(bf16[1,1,2,2,1,24,1280]{6,5,4,3,2,1,0:T(8,128)(2,1)S(1)} %dynamic-slice_convert_fusion.5.refs_2_), channel_id=1, source_target_pairs={{0,1},{1,0},{2,3},{3,2},{4,5},{5,4},{6,7},{7,6},{8,9},{9,8},{10,11... | collective-permute-start | bytes 737288 | tf_op jit(solution)/shard_map/ppermute | solution.py:813
  283.7 0.7 copy-start.15
  284.4 3.9 %copy-start.16 = (bf16[1,1,2,1,1,24,3840]{6,5,4,3,2,1,0:T(8,128)(2,1)S(1)}, bf16[1,1,2,1,1,24,3840]{6,5,4,3,2,1,0:T(8,128)(2,1)}, u32[]{:S(2)}) copy-start(bf16[1,1,2,1,1,24,3840]{6,5,4,3,2,1,0:T(8,128)(2,1)} %get-tuple-element.133) | copy-start | bytes 1105924
  285.5 21.7 %collective-permute-start.28 = (bf16[1,1,1,1,1,24,3072]{6,5,4,3,2,1,0:T(8,128)(2,1)S(1)}, bf16[1,1,1,1,1,24,3072]{6,5,4,3,2,1,0:T(8,128)(2,1)S(1)}, u32[]{:S(2)}, u32[]{:S(2)}) collective-permute-start(bf16[1,1,1,1,1,24,3072]{6,5,4,3,2,1,0:T(8,128)(2,1)S(1)} %dynamic-slice_convert_fusion.7), channel_id=1, source_target_pairs={{0,4},{1,5},{2,6},{3,7},{4,0},{5,1},{6,2},{7,3},{8,12},{9,13},{10,... | collective-permute-start | bytes 442376 | tf_op jit(solution)/shard_map/ppermute | solution.py:813
  288.4 1.8 copy-start.6
  288.5 5.4 %copy-start.8 = (f32[1,1,2,2,2,24,1280]{6,5,4,3,2,1,0:T(8,128)S(1)}, f32[1,1,2,2,2,24,1280]{6,5,4,3,2,1,0:T(8,128)}, u32[]{:S(2)}) copy-start(f32[1,1,2,2,2,24,1280]{6,5,4,3,2,1,0:T(8,128)} %copy-done.7) | copy-start | bytes 2949124
  288.5 18.8 %collective-permute-start.27 = (bf16[1,1,1,1,1,24,3840]{6,5,4,3,2,1,0:T(8,128)(2,1)S(1)}, bf16[1,1,1,1,1,24,3840]{6,5,4,3,2,1,0:T(8,128)(2,1)S(1)}, u32[]{:S(2)}, u32[]{:S(2)}) collective-permute-start(bf16[1,1,1,1,1,24,3840]{6,5,4,3,2,1,0:T(8,128)(2,1)S(1)} %dynamic-slice_convert_fusion.6), channel_id=1, source_target_pairs={{0,4},{1,5},{2,6},{3,7},{4,0},{5,1},{6,2},{7,3},{8,12},{9,13},{10,... | collective-permute-start | bytes 552968 | tf_op jit(solution)/shard_map/ppermute | solution.py:813
  291.2 9.3 %collective-permute-start.23 = (bf16[1,1,2,1,1,24,1280]{6,5,4,3,2,1,0:T(8,128)(2,1)S(1)}, bf16[1,1,2,1,1,24,1280]{6,5,4,3,2,1,0:T(8,128)(2,1)S(1)}, u32[]{:S(2)}, u32[]{:S(2)}) collective-permute-start(bf16[1,1,2,1,1,24,1280]{6,5,4,3,2,1,0:T(8,128)(2,1)S(1)} %dynamic-slice_convert_fusion.8), channel_id=1, source_target_pairs={{0,2},{1,3},{2,0},{3,1},{4,6},{5,7},{6,4},{7,5},{8,10},{9,11},{10,... | collective-permute-start | bytes 368648 | tf_op jit(solution)/shard_map/ppermute | solution.py:813
  295.0 8.8 %collective-permute-start.19 = (bf16[1,1,2,1,1,24,1280]{6,5,4,3,2,1,0:T(8,128)(2,1)S(1)}, bf16[1,1,2,1,1,24,1280]{6,5,4,3,2,1,0:T(8,128)(2,1)S(1)}, u32[]{:S(2)}, u32[]{:S(2)}) collective-permute-start(bf16[1,1,2,1,1,24,1280]{6,5,4,3,2,1,0:T(8,128)(2,1)S(1)} %dynamic-slice_convert_fusion.9), channel_id=1, source_target_pairs={{0,2},{1,3},{2,0},{3,1},{4,6},{5,7},{6,4},{7,5},{8,10},{9,11},{10,... | collective-permute-start | bytes 368648 | tf_op jit(solution)/shard_map/ppermute | solution.py:813
  300.6 6.7 %copy-start.23 = (bf16[1,1,1,1,1,24,1280]{6,5,4,3,2,1,0:T(8,128)(2,1)}, bf16[1,1,1,1,1,24,1280]{6,5,4,3,2,1,0:T(8,128)(2,1)S(1)}, u32[]{:S(2)}) copy-start(bf16[1,1,1,1,1,24,1280]{6,5,4,3,2,1,0:T(8,128)(2,1)S(1)} %dynamic-slice_convert_fusion.10.refs_3_) | copy-start | bytes 184324
  300.6 10.5 %collective-permute-start.24 = (bf16[1,1,1,1,1,24,1280]{6,5,4,3,2,1,0:T(8,128)(2,1)S(1)}, bf16[1,1,1,1,1,24,1280]{6,5,4,3,2,1,0:T(8,128)(2,1)S(1)}, u32[]{:S(2)}, u32[]{:S(2)}) collective-permute-start(bf16[1,1,1,1,1,24,1280]{6,5,4,3,2,1,0:T(8,128)(2,1)S(1)} %dynamic-slice_convert_fusion.10.refs_3_), channel_id=1, source_target_pairs={{0,4},{1,5},{2,6},{3,7},{4,0},{5,1},{6,2},{7,3},{8,12},{9,13},{10,... | collective-permute-start | bytes 184328 | tf_op jit(solution)/shard_map/ppermute | solution.py:813
  303.9 3.5 %copy-start.24 = (bf16[1,1,1,1,1,24,1280]{6,5,4,3,2,1,0:T(8,128)(2,1)}, bf16[1,1,1,1,1,24,1280]{6,5,4,3,2,1,0:T(8,128)(2,1)S(1)}, u32[]{:S(2)}) copy-start(bf16[1,1,1,1,1,24,1280]{6,5,4,3,2,1,0:T(8,128)(2,1)S(1)} %dynamic-slice_convert_fusion.11.refs_2_) | copy-start | bytes 184324
  303.9 7.3 %collective-permute-start.20 = (bf16[1,1,1,1,1,24,1280]{6,5,4,3,2,1,0:T(8,128)(2,1)S(1)}, bf16[1,1,1,1,1,24,1280]{6,5,4,3,2,1,0:T(8,128)(2,1)S(1)}, u32[]{:S(2)}, u32[]{:S(2)}) collective-permute-start(bf16[1,1,1,1,1,24,1280]{6,5,4,3,2,1,0:T(8,128)(2,1)S(1)} %dynamic-slice_convert_fusion.11.refs_2_), channel_id=1, source_target_pairs={{0,4},{1,5},{2,6},{3,7},{4,0},{5,1},{6,2},{7,3},{8,12},{9,13},{10,... | collective-permute-start | bytes 184328 | tf_op jit(solution)/shard_map/ppermute | solution.py:813
  307.3 0.7 copy-start.22
  308.0 0.7 copy-start.20
  311.1 0.6 copy-start.25
  311.1 0.6 copy-start.26
Sparse Core Ops, SparseCore 0:
  11.0 93.5 all-gather.3
  231.7 56.3 all-gather.5
where the time goes:
time: 323 us; the launch traced here: 321 us
  Pallas kernels  190 us (59%)
  waiting for transfers between devices  41 us (13%)
  starting transfers between devices  31.9 us (10%)
  local copies, waits for them, and re-layouts  20.9 us (6%)
  other arithmetic  18.9 us (6%)
  between operations  18.1 us (6%)
    pallas_call x1, Pallas kernels, middle(): pl.pallas_call(middle_kernel, grid=(steps + 1,), out_shape=(shaped((GH, G...  68.1 us
    ppermute x29, waiting for transfers between devices, swap(): return lax.ppermute(value, AXES, [(i, i ^ bit) for i in range(self.count)])  41 us
    pallas_call x2, Pallas kernels, backward(): pl.pallas_call(backward_kernel, grid=(count,), out_shape=(shaped((count *...  31.9 us
    ppermute x29, starting transfers between devices, swap(): return lax.ppermute(value, AXES, [(i, i ^ bit) for i in range(self.count)])  31.9 us
    pallas_call x1, Pallas kernels, forward(): pl.pallas_call(forward_kernel, grid=(WINDOWS,), out_shape=(shaped((WINDOW...  31.6 us
    pallas_call x1, Pallas kernels, end(): pl.pallas_call(end_kernel, out_shape=(shaped((GH, GW, D), bf16), shaped((...  16.1 us
    pallas_call x1, Pallas kernels, attention_weights(): pl.pallas_call(attention_weights_kernel, grid=(1,), out_shape=(shaped((D...  13.6 us
    unnamed x62, local copies, waits for them, and re-layouts  11.9 us
  transfers between devices with their start and end apart: 31, of which 11 were waited for; matrix products, arithmetic and copies ran while one was open for 9% of the time, Pallas kernels for 35%

commit v1 on v0

--- a/solution.py
+++ b/solution.py
@@ -718,7 +718,7 @@
         out_specs=(pl.BlockSpec((TOK, 3 * D), lambda i: (i, 0)), whole((8, D)), whole((256, 128)), FLAG),
         scratch_shapes=[pltpu.VMEM((TOK, D), bf16)],
         compiler_params=params(1),
-        cost_estimate=pl.CostEstimate(flops=6_000_000_000 * count, bytes_accessed=9_000_000, transcendentals=0),
+        cost_estimate=pl.CostEstimate(flops=1_000_000_000, bytes_accessed=2_000_000, transcendentals=0),
         name="attend_back",
     )(packed, soft, att, gbr, two, table, hot, *before)
 
@@ -737,7 +737,7 @@
         out_specs=(whole((D // 2, 3 * D + 256)),) * 2 + (FLAG,),
         scratch_shapes=[pltpu.VMEM((WINDOWS * TOK, 3 * D), bf16), pltpu.SemaphoreType.DMA((3 * len(CALLS),))],
         compiler_params=params(1),
-        cost_estimate=pl.CostEstimate(flops=25_000_000_000, bytes_accessed=18_000_000, transcendentals=0),
+        cost_estimate=pl.CostEstimate(flops=1_000_000_000, bytes_accessed=2_000_000, transcendentals=0),
         name="attend_weights",
     )(core, *sums, tiles, *gpacked, *gbias, *before)
 
@@ -756,7 +756,7 @@
             pltpu.SemaphoreType.DMA((len(CALLS) + 2,)),
         ],
         compiler_params=params(),
-        cost_estimate=pl.CostEstimate(flops=12_000_000_000, bytes_accessed=17_000_000, transcendentals=0),
+        cost_estimate=pl.CostEstimate(flops=1_000_000_000, bytes_accessed=2_000_000, transcendentals=0),
         name="end",
     )(images, gbr, one, two, vec, *gpacked, *gtab, *before)
 
@@ -1027,7 +1027,7 @@
     feed, flag = links.narrow(feed, (first[1], second[1]), (FF + D, FF), [flag])
     all_tables = lax.all_gather(tables, AXES, axis=0, tiled=False)
     gin_k, gin_s, flag = attention_weights(core, (sums1, sums2, gupb), tiles, gpacked, [b[1] for b in back], flag)
-    *recv, gin_s = links.tie([f[0][-1] for f in feed] + [gin_s], [flag])
+    recv = links.tie([f[0][-1] for f in feed], [flag])
     feed = [(f[0][:-1] + [r], f[1], f[2]) for f, r in zip(feed, recv)]
     gin = links.cut(gin_k, gin_s)
     feed = [links.halve(links.own_part(f), at) for f, at in zip(feed, (first[2], second[2]))]

time: 323 us -> 321 us (level)
  transfers between devices with their start and end apart: 31 -> 31, of which waited for: 11 -> 11; matrix products, arithmetic and copies ran while one was open for 9% -> 10% of each run, Pallas kernels for 35% -> 34%
where the time goes in v1:
time: 321 us; the launch traced here: 319 us
  Pallas kernels  190 us (59%)
  waiting for transfers between devices  39 us (12%)
  starting transfers between devices  30.9 us (10%)
  local copies, waits for them, and re-layouts  20.4 us (6%)
  other arithmetic  20.4 us (6%)
  between operations  18.2 us (6%)
    pallas_call x1, Pallas kernels, middle(): pl.pallas_call(middle_kernel, grid=(steps + 1,), out_shape=(shaped((GH, G...  68.1 us
    ppermute x29, waiting for transfers between devices, swap(): return lax.ppermute(value, AXES, [(i, i ^ bit) for i in range(self.count)])  39 us
    pallas_call x2, Pallas kernels, backward(): pl.pallas_call(backward_kernel, grid=(count,), out_shape=(shaped((count *...  31.9 us
    pallas_call x1, Pallas kernels, forward(): pl.pallas_call(forward_kernel, grid=(WINDOWS,), out_shape=(shaped((WINDOW...  31.6 us
    ppermute x29, starting transfers between devices, swap(): return lax.ppermute(value, AXES, [(i, i ^ bit) for i in range(self.count)])  30.8 us
    pallas_call x1, Pallas kernels, end(): pl.pallas_call(end_kernel, out_shape=(shaped((GH, GW, D), bf16), shaped((...  16.1 us
    pallas_call x1, Pallas kernels, attention_weights(): pl.pallas_call(attention_weights_kernel, grid=(1,), out_shape=(shaped((D...  13.5 us
    unnamed x62, local copies, waits for them, and re-layouts  11.4 us
  transfers between devices with their start and end apart: 31, of which 11 were waited for; matrix products, arithmetic and copies ran while one was open for 10% of the time, Pallas kernels for 34%

profile of v1, /device:TPU:0, one launch (start us, length us, event | category | flops | bytes accessed | tf_op | source)
XLA Modules:
  0.0 318.8 jit_solution(15344118409890928800)
XLA Ops:
  7.3 2.0 pack_feed.1
  9.3 0.8 slice.15
  10.1 0.8 fusion.12
  10.9 4.1 %collective-permute-start = (bf16[1,1,1,1,1,24,1536]{6,5,4,3,2,1,0:T(8,128)(2,1)S(1)}, bf16[1,1,1,1,1,24,1536]{6,5,4,3,2,1,0:T(8,128)(2,1)S(1)}, u32[]{:S(2)}, u32[]{:S(2)}) collective-permute-start(bf16[1,1,1,1,1,24,1536]{6,5,4,3,2,1,0:T(8,128)(2,1)S(1)} %get-tuple-element.163), channel_id=1, source_target_pairs={{0,4},{1,5},{2,6},{3,7},{4,0},{5,1},{6,2},{7,3},{8,12},{9,13},{10,... | collective-permute-start | bytes 221192 | tf_op jit(solution)/shard_map/ppermute | solution.py:813
  15.0 1.4 stack.53.eight_ref
  16.3 1.7 pack.1
  18.1 1.5 copy.61
  19.6 0.8 copy.62
  20.4 0.8 copy.67.valid_ref
  21.9 1.9 collective-permute-start.1
  23.8 1.1 collective-permute-done.2
  25.0 1.0 fusion.7
  26.4 4.9 %collective-permute-done.1 = bf16[1,1,2,1,1,24,1536]{6,5,2,4,3,1,0:T(8,128)(2,1)S(1)} collective-permute-done((bf16[1,1,2,1,1,24,1536]{6,5,2,4,3,1,0:T(8,128)(2,1)S(1)}, bf16[1,1,2,1,1,24,1536]{6,5,2,4,3,1,0:T(8,128)(2,1)S(1)}, u32[]{:S(2)}, u32[]{:S(2)}) %collective-permute-start.1) | collective-permute-done | bytes 147488 | tf_op jit(solution)/shard_map/ppermute | solution.py:813
  32.8 1.8 collective-permute-start.4
  34.6 1.8 collective-permute-done.3
  36.5 1.6 collective-permute-start.5
  38.2 0.7 copy.69.refs_1_
  39.0 4.9 %weigh.1 = (f32[992,768]{1,0:T(8,128)}, bf16[992,768]{1,0:T(8,128)(2,1)}, bf16[128,256]{1,0:T(8,128)(2,1)}, bf16[128,256]{1,0:T(8,128)(2,1)}, s32[1]{0:T(128)}) custom-call(s32[1]{0:T(128)S(6)} %copy.88.count_ref, bf16[26,38,768]{2,1,0:T(8,128)(2,1)} %bitcast.131, s32[300,2]{1,0:T(8,128)} %bitcast.140, s32[300,2]{1,0:T(8,128)} %bitcast.141, ...), custom_call_target="tpu_custom_call" | custom-call | flops 30000000 | bytes 6000000 | tf_op jit(solution)/shard_map/weigh/pallas_call | solution.py:593
  45.2 0.8 maximum_select_fusion.5
  46.2 1.6 collective-permute-start.6
  48.0 1.4 collective-permute-start.7
  49.4 1.2 fusion.6
  50.6 4.9 %begin.1 = (f32[84,16,768]{2,1,0:T(8,128)}, s32[1]{0:T(128)}) custom-call(bf16[26,38,768]{2,1,0:T(8,128)(2,1)} %bitcast.121, bf16[2,1,2,2,1,24,1536]{6,5,4,3,2,1,0:T(8,128)(2,1)} %copy-done.1, bf16[1,1,2,2,2,24,1664]{6,5,4,3,2,1,0:T(8,128)(2,1)} %copy-done.13), custom_call_target="tpu_custom_call" | custom-call | flops 30000000 | bytes 6000000 | tf_op jit(solution)/shard_map/begin/pallas_call | solution.py:581
  56.8 1.3 fusion.4
  58.1 5.3 %collective-permute-done.6 = bf16[1,1,2,2,2,24,1664]{6,5,4,3,2,1,0:T(8,128)(2,1)S(1)} collective-permute-done((bf16[1,1,2,2,2,24,1664]{6,5,4,3,2,1,0:T(8,128)(2,1)S(1)}, bf16[1,1,2,2,2,24,1664]{6,5,4,3,2,1,0:T(8,128)(2,1)S(1)}, u32[]{:S(2)}, u32[]{:S(2)}) %collective-permute-start.6) | collective-permute-done | bytes 639008 | tf_op jit(solution)/shard_map/ppermute | solution.py:813
  63.4 1.4 maximum_select_fusion.1
  64.8 1.9 collective-permute-done.7
  66.7 3.0 fusion.1
  70.2 1.3 maximum_select_fusion.refs_0_
  71.5 1.2 collective-permute-done.9
  72.7 1.1 copy-done.29
  73.8 31.6 %attend.1 = (bf16[1344,768]{1,0:T(8,128)(2,1)}, bf16[1344,2304]{1,0:T(8,128)(2,1)}, bf16[72,224,224]{2,1,0:T(8,128)(2,1)}, bf16[1344,768]{1,0:T(8,128)(2,1)}, f3...) custom-call(s32[5]{0:T(128)} %stack.59.places_ref.places, ...), custom_call_target="tpu_custom_call" | custom-call | flops 30000001024 | bytes 28000000 | tf_op jit(solution)/shard_map/attend/pallas_call | solution.py:612
  105.4 68.1 %feed.1 = (bf16[26,38,768]{2,1,0:T(8,128)(2,1)}, bf16[84,16,768]{2,1,0:T(8,128)(2,1)}, bf16[384,3840]{1,0:T(8,128)(2,1)}, bf16[384,3840]{1,0:T(8,128)(2,1)}, bf1...) custom-call(s32[1]{0:T(128)} %bitcast.core_ref, ...), custom_call_target="tpu_custom_call" | custom-call | flops 49999998976 | bytes 36000000 | tf_op jit(solution)/shard_map/feed/pallas_call | solution.py:646
  174.1 11.8 %attend_back.2 = (bf16[448,2304]{1,0:T(8,128)(2,1)}, f32[8,768]{1,0:T(8,128)}, f32[256,128]{1,0:T(8,128)}, s32[1]{0:T(128)}) custom-call(bf16[1344,2304]{1,0:T(8,128)(2,1)} %get-tuple-element.95.packed_ref, bf16[72,224,224]{2,1,0:T(8,128)(2,1)} %get-tuple-element.96.soft_ref, bf16[1344,768]{1,0:T(8,128)(2,1)} %get-tuple-element.90.refs_1_.att_ref, ...), custom_call_target="tpu_custom_call" | custom-call | flops 1000000000 | bytes 2000000 | tf_op jit(solution)/shard_map/attend_back/pallas_call | solution.py:699
  185.9 1.7 copy-done
  187.6 5.2 %narrow.2 = (bf16[1,1,2,2,2,24,3840]{6,5,4,3,2,1,0:T(8,128)(2,1)}, bf16[2,1,2,2,1,24,3072]{6,5,4,3,2,1,0:T(8,128)(2,1)}, s32[1]{0:T(128)}) custom-call(s32[5]{0:T(128)} %stack.59.places_ref.places, bf16[2,1,2,2,2,24,3840]{6,5,4,3,2,1,0:T(8,128)(2,1)} %bitcast.112, bf16[2,1,2,2,2,24,3840]{6,5,4,3,2,1,0:T(8,128)(2,1)} %bitcast.115, ...), custom_call_target="tpu_custom_call" | custom-call | flops 5308416 | bytes 10616832 | tf_op jit(solution)/shard_map/narrow/pallas_call | solution.py:921
  192.8 1.5 collective-permute-start.12
  194.3 1.1 collective-permute-start.13
  195.3 20.1 %attend_back.3 = (bf16[896,2304]{1,0:T(8,128)(2,1)}, f32[8,768]{1,0:T(8,128)}, f32[256,128]{1,0:T(8,128)}, s32[1]{0:T(128)}) custom-call(bf16[1344,2304]{1,0:T(8,128)(2,1)} %get-tuple-element.95.packed_ref, bf16[72,224,224]{2,1,0:T(8,128)(2,1)} %get-tuple-element.96.soft_ref, bf16[1344,768]{1,0:T(8,128)(2,1)} %get-tuple-element.90.refs_1_.att_ref, ...), custom_call_target="tpu_custom_call" | custom-call | flops 1000000000 | bytes 2000000 | tf_op jit(solution)/shard_map/attend_back/pallas_call | solution.py:699
  215.4 16.1 %end.1 = (bf16[26,38,768]{2,1,0:T(8,128)(2,1)}, f32[8,768]{1,0:T(8,128)}, f32[64,128]{1,0:T(8,128)}, s32[1]{0:T(128)}) custom-call(bf16[26,38,768]{2,1,0:T(8,128)(2,1)} %bitcast.123, bf16[84,16,768]{2,1,0:T(8,128)(2,1)} %get-tuple-element.92.gbr_ref, bf16[768,1664]{1,0:T(8,128)(2,1)} %get-tuple-element.93.one_ref, ...), custom_call_target="tpu_custom_call" | custom-call | flops 1000000000 | bytes 2000000 | tf_op jit(solution)/shard_map/end/pallas_call | solution.py:746
  231.6 1.0 copy-done.11
  233.1 4.7 %narrow.3 = (bf16[1,1,2,2,1,24,3840]{6,5,4,3,2,1,0:T(8,128)(2,1)}, bf16[1,1,2,2,1,24,3072]{6,5,4,3,2,1,0:T(8,128)(2,1)}, s32[1]{0:T(128)}) custom-call(s32[5]{0:T(128)} %stack.59.places_ref.places, bf16[2,1,2,2,2,24,3840]{6,5,4,3,2,1,0:T(8,128)(2,1)} %bitcast.113, bf16[2,1,2,2,2,24,3840]{6,5,4,3,2,1,0:T(8,128)(2,1)} %bitcast.116, ...), custom_call_target="tpu_custom_call" | custom-call | flops 2654208 | bytes 5308416 | tf_op jit(solution)/shard_map/narrow/pallas_call | solution.py:921
  237.8 1.0 collective-permute-start.23
  239.5 13.5 %attend_weights.1 = (bf16[384,2560]{1,0:T(8,128)(2,1)}, bf16[384,2560]{1,0:T(8,128)(2,1)}, s32[1]{0:T(128)}) custom-call(s32[1]{0:T(128)} %bitcast.core_ref, f32[8,768]{1,0:T(8,128)} %get-tuple-element.110.sums1_ref, f32[8,768]{1,0:T(8,128)} %get-tuple-element.111.sums2_ref, f32[8,768]{1,0:T(8,128)} %get-tuple-element.112.gupb_ref, ...), custom_call_target="tpu_custom_call" | custom-call | flops 1000000000 | bytes 2000000 | tf_op jit(solution)/shard_map/attend_weights/pallas_call | solution.py:727
  253.1 0.9 collective-permute-done.24.refs_1_
  254.0 2.4 collective-permute-done.23.refs_0_
  256.4 0.8 copy-done.9
  257.9 1.9 convert_add_fusion.3
  259.9 2.6 collective-permute-start.26
  262.5 1.8 convert_add_fusion.2
  264.5 2.1 convert_add_fusion
  267.9 11.2 %collective-permute-done.19 = bf16[2,1,2,2,1,24,1280]{6,5,4,3,2,1,0:T(8,128)(2,1)S(1)} collective-permute-done((bf16[2,1,2,2,1,24,1280]{6,5,4,3,2,1,0:T(8,128)(2,1)S(1)}, bf16[2,1,2,2,1,24,1280]{6,5,4,3,2,1,0:T(8,128)(2,1)S(1)}, u32[]{:S(2)}, u32[]{:S(2)}) %collective-permute-start.19) | collective-permute-done | bytes 491552 | tf_op jit(solution)/shard_map/ppermute | solution.py:813
  280.3 0.9 copy-done.7
  282.6 1.1 convert_add_fusion.7
  283.7 2.9 collective-permute-start.28
  286.9 0.8 dynamic-slice_bitcast_fusion.refs_0_
  288.4 1.0 convert_add_fusion.8
  289.4 3.2 %collective-permute-start.21 = (bf16[1,1,2,1,1,24,1280]{6,5,4,3,2,1,0:T(8,128)(2,1)S(1)}, bf16[1,1,2,1,1,24,1280]{6,5,4,3,2,1,0:T(8,128)(2,1)S(1)}, u32[]{:S(2)}, u32[]{:S(2)}) collective-permute-start(bf16[1,1,2,1,1,24,1280]{6,5,4,3,2,1,0:T(8,128)(2,1)S(1)} %dynamic-slice_convert_fusion.8), channel_id=1, source_target_pairs={{0,2},{1,3},{2,0},{3,1},{4,6},{5,7},{6,4},{7,5},{8,10},{9,11},{10,... | collective-permute-start | bytes 368648 | tf_op jit(solution)/shard_map/ppermute | solution.py:813
  292.7 1.0 convert_add_fusion.9
  293.8 5.1 %collective-permute-done.21 = bf16[1,1,2,1,1,24,1280]{6,5,4,3,2,1,0:T(8,128)(2,1)S(1)} collective-permute-done((bf16[1,1,2,1,1,24,1280]{6,5,4,3,2,1,0:T(8,128)(2,1)S(1)}, bf16[1,1,2,1,1,24,1280]{6,5,4,3,2,1,0:T(8,128)(2,1)S(1)}, u32[]{:S(2)}, u32[]{:S(2)}) %collective-permute-start.21) | collective-permute-done | bytes 122912 | tf_op jit(solution)/shard_map/ppermute | solution.py:813
  298.9 1.7 collective-permute-start.22
  300.6 3.1 collective-permute-done.17
  306.5 2.5 unpack_feed.1
  309.6 2.2 unpack_in.1
  (133 shorter events, 14.3 us)
Async XLA Ops:
  7.2 12.4 %copy-start.27 = (s32[1,300,2]{1,2,0:T(2,128)S(1)}, s32[1,300,2]{1,2,0:T(2,128)}, u32[]{:S(2)}) copy-start(s32[1,300,2]{1,2,0:T(2,128)} %param.26) | copy-start | bytes 7204
  7.2 13.2 %copy-start.28 = (s32[1,300]{1,0:T(1,128)S(1)}, s32[1,300]{1,0:T(1,128)}, u32[]{:S(2)}) copy-start(s32[1,300]{1,0:T(1,128)} %param.27) | copy-start | bytes 3604
  7.2 98.2 %all-gather.4.cloned.1.call-start = ((), (), s32[]{:S(2)}) async-start(), calls=%async_computation | async-start | bytes 9732096 | tf_op jit(solution)/shard_map/all_gather | solution.py:993
  9.2 299.7 %all-gather.6.cloned.1.call-start = ((), (), s32[]{:S(2)}) async-start(), calls=%async_computation.1 | async-start | bytes 1081344 | tf_op jit(solution)/shard_map/all_gather | solution.py:1028
  10.9 11.0 %collective-permute-start = (bf16[1,1,1,1,1,24,1536]{6,5,4,3,2,1,0:T(8,128)(2,1)S(1)}, bf16[1,1,1,1,1,24,1536]{6,5,4,3,2,1,0:T(8,128)(2,1)S(1)}, u32[]{:S(2)}, u32[]{:S(2)}) collective-permute-start(bf16[1,1,1,1,1,24,1536]{6,5,4,3,2,1,0:T(8,128)(2,1)S(1)} %get-tuple-element.163), channel_id=1, source_target_pairs={{0,4},{1,5},{2,6},{3,7},{4,0},{5,1},{6,2},{7,3},{8,12},{9,13},{10,... | collective-permute-start | bytes 221192 | tf_op jit(solution)/shard_map/ppermute | solution.py:813
  18.0 8.3 %copy-start.21 = (bf16[24,1664]{1,0:T(8,128)(2,1)S(1)}, bf16[24,1664]{1,0:T(8,128)(2,1)}, u32[]{:S(2)}) copy-start(bf16[24,1664]{1,0:T(8,128)(2,1)} %pack.1) | copy-start | bytes 239620
  18.0 6.9 %collective-permute-start.2 = (bf16[1,1,1,1,1,24,1664]{6,5,4,3,2,1,0:T(8,128)(2,1)}, bf16[1,1,1,1,1,24,1664]{6,5,4,3,2,1,0:T(8,128)(2,1)S(1)}, u32[]{:S(2)}, u32[]{:S(2)}) collective-permute-start(bf16[1,1,1,1,1,24,1664]{6,5,4,3,2,1,0:T(8,128)(2,1)} %bitcast.137), channel_id=1, source_target_pairs={{0,4},{1,5},{2,6},{3,7},{4,0},{5,1},{6,2},{7,3},{8,12},{9,13},{10,... | collective-permute-start | bytes 239624 | tf_op jit(solution)/shard_map/ppermute | solution.py:813
  21.9 9.4 %collective-permute-start.1 = (bf16[1,1,2,1,1,24,1536]{6,5,2,4,3,1,0:T(8,128)(2,1)S(1)}, bf16[1,1,2,1,1,24,1536]{6,5,2,4,3,1,0:T(8,128)(2,1)S(1)}, u32[]{:S(2)}, u32[]{:S(2)}) collective-permute-start(bf16[1,1,2,1,1,24,1536]{6,5,2,4,3,1,0:T(8,128)(2,1)S(1)} %fusion.8), channel_id=1, source_target_pairs={{0,2},{1,3},{2,0},{3,1},{4,6},{5,7},{6,4},{7,5},{8,10},{9,11},{10,... | collective-permute-start | bytes 442376 | tf_op jit(solution)/shard_map/ppermute | solution.py:813
  26.0 10.5 %collective-permute-start.3 = (bf16[1,1,2,1,1,24,1664]{6,5,2,4,3,1,0:T(8,128)(2,1)S(1)}, bf16[1,1,2,1,1,24,1664]{6,5,2,4,3,1,0:T(8,128)(2,1)S(1)}, u32[]{:S(2)}, u32[]{:S(2)}) collective-permute-start(bf16[1,1,2,1,1,24,1664]{6,5,2,4,3,1,0:T(8,128)(2,1)S(1)} %fusion.7), channel_id=1, source_target_pairs={{0,2},{1,3},{2,0},{3,1},{4,6},{5,7},{6,4},{7,5},{8,10},{9,11},{10,... | collective-permute-start | bytes 479240 | tf_op jit(solution)/shard_map/ppermute | solution.py:813
  32.8 15.0 %collective-permute-start.4 = (bf16[1,1,2,2,1,24,1536]{6,5,3,2,4,1,0:T(8,128)(2,1)}, bf16[1,1,2,2,1,24,1536]{6,5,3,2,4,1,0:T(8,128)(2,1)S(1)}, u32[]{:S(2)}, u32[]{:S(2)}) collective-permute-start(bf16[1,1,2,2,1,24,1536]{6,5,3,2,4,1,0:T(8,128)(2,1)} %copy.70), channel_id=1, source_target_pairs={{0,16},{1,17},{2,18},{3,19},{4,20},{5,21},{6,22},{7,23},{8,24},{9,... | collective-permute-start | bytes 884744 | tf_op jit(solution)/shard_map/ppermute | solution.py:813
  36.5 9.5 %collective-permute-start.5 = (bf16[1,1,2,2,1,24,1664]{6,5,2,3,4,1,0:T(8,128)(2,1)S(1)}, bf16[1,1,2,2,1,24,1664]{6,5,2,3,4,1,0:T(8,128)(2,1)S(1)}, u32[]{:S(2)}, u32[]{:S(2)}) collective-permute-start(bf16[1,1,2,2,1,24,1664]{6,5,2,3,4,1,0:T(8,128)(2,1)S(1)} %maximum_select_fusion.3), channel_id=1, source_target_pairs={{0,1},{1,0},{2,3},{3,2},{4,5},{5,4},{6,7},{7,6},{8,9},{9,8},{10,11... | collective-permute-start | bytes 958472 | tf_op jit(solution)/shard_map/ppermute | solution.py:813
  46.2 4.3 %copy-start.13 = (bf16[1,1,2,2,2,24,1664]{6,5,4,3,2,1,0:T(8,128)(2,1)}, bf16[1,1,2,2,2,24,1664]{6,5,4,3,2,1,0:T(8,128)(2,1)S(1)}, u32[]{:S(2)}) copy-start(bf16[1,1,2,2,2,24,1664]{6,5,4,3,2,1,0:T(8,128)(2,1)S(1)} %copy_select_fusion.refs_1_) | copy-start | bytes 1916932
  46.2 17.2 %collective-permute-start.6 = (bf16[1,1,2,2,2,24,1664]{6,5,4,3,2,1,0:T(8,128)(2,1)S(1)}, bf16[1,1,2,2,2,24,1664]{6,5,4,3,2,1,0:T(8,128)(2,1)S(1)}, u32[]{:S(2)}, u32[]{:S(2)}) collective-permute-start(bf16[1,1,2,2,2,24,1664]{6,5,4,3,2,1,0:T(8,128)(2,1)S(1)} %copy_select_fusion.refs_1_), channel_id=1, source_target_pairs={{0,16},{1,17},{2,18},{3,19},{4,20},{5,21},{6,22},{7,23},{8,24},{9,... | collective-permute-start | bytes 1916936 | tf_op jit(solution)/shard_map/ppermute | solution.py:813
  47.9 1.5 copy-start.17
  48.0 2.6 copy-start.1
  48.0 18.7 %collective-permute-start.7 = (bf16[2,1,2,2,1,24,1536]{6,5,4,3,2,1,0:T(8,128)(2,1)S(1)}, bf16[2,1,2,2,1,24,1536]{6,5,4,3,2,1,0:T(8,128)(2,1)}, u32[]{:S(2)}, u32[]{:S(2)}) collective-permute-start(bf16[2,1,2,2,1,24,1536]{6,5,4,3,2,1,0:T(8,128)(2,1)S(1)} %fusion.5.refs_0_), channel_id=1, source_target_pairs={{0,1},{1,0},{2,3},{3,2},{4,5},{5,4},{6,7},{7,6},{8,9},{9,8},{10,11... | collective-permute-start | bytes 1769480 | tf_op jit(solution)/shard_map/ppermute | solution.py:813
  58.1 8.6 %copy-start.2 = (bf16[2,1,2,2,1,24,1536]{6,5,4,3,2,1,0:T(8,128)(2,1)S(1)}, bf16[2,1,2,2,1,24,1536]{6,5,4,3,2,1,0:T(8,128)(2,1)}, u32[]{:S(2)}) copy-start(bf16[2,1,2,2,1,24,1536]{6,5,4,3,2,1,0:T(8,128)(2,1)} %copy-done.1) | copy-start | bytes 1769476
  64.8 7.9 %collective-permute-start.8 = (bf16[2,1,2,2,2,24,1664]{6,5,4,3,2,1,0:T(8,128)(2,1)}, bf16[2,1,2,2,2,24,1664]{6,5,4,3,2,1,0:T(8,128)(2,1)}, u32[]{:S(2)}, u32[]{:S(2)}) collective-permute-start(bf16[2,1,2,2,2,24,1664]{6,5,4,3,2,1,0:T(8,128)(2,1)} %maximum_select_fusion.1), channel_id=1, source_target_pairs={{0,8},{1,9},{2,10},{3,11},{4,12},{5,13},{6,14},{7,15},{8,0},{9,1},... | collective-permute-start | bytes 3833864 | tf_op jit(solution)/shard_map/ppermute | solution.py:813
  69.6 3.1 collective-permute-start.9
  72.7 1.1 copy-start.29
  173.6 12.4 %collective-permute-start.10 = (bf16[384,3840]{1,0:T(8,128)(2,1)}, bf16[384,3840]{1,0:T(8,128)(2,1)S(1)}, u32[]{:S(2)}, u32[]{:S(2)}) collective-permute-start(bf16[384,3840]{1,0:T(8,128)(2,1)} %get-tuple-element.100), channel_id=1, source_target_pairs={{0,8},{1,9},{2,10},{3,11},{4,12},{5,13},{6,14},{7,15},{8,0},{9,1},... | collective-permute-start | bytes 8847368 | tf_op jit(solution)/shard_map/ppermute | solution.py:813
  173.8 12.1 %collective-permute-start.11 = (bf16[384,3072]{1,0:T(8,128)(2,1)}, bf16[384,3072]{1,0:T(8,128)(2,1)}, u32[]{:S(2)}, u32[]{:S(2)}) collective-permute-start(bf16[384,3072]{1,0:T(8,128)(2,1)} %get-tuple-element.102), channel_id=1, source_target_pairs={{0,8},{1,9},{2,10},{3,11},{4,12},{5,13},{6,14},{7,15},{8,0},{9,1},... | collective-permute-start | bytes 7077896 | tf_op jit(solution)/shard_map/ppermute | solution.py:813
  185.9 1.7 copy-start
  192.8 38.8 %collective-permute-start.12 = (bf16[1,1,2,2,2,24,3840]{6,5,4,3,2,1,0:T(8,128)(2,1)}, bf16[1,1,2,2,2,24,3840]{6,5,4,3,2,1,0:T(8,128)(2,1)S(1)}, u32[]{:S(2)}, u32[]{:S(2)}) collective-permute-start(bf16[1,1,2,2,2,24,3840]{6,5,4,3,2,1,0:T(8,128)(2,1)} %get-tuple-element.116), channel_id=1, source_target_pairs={{0,16},{1,17},{2,18},{3,19},{4,20},{5,21},{6,22},{7,23},{8,24},{9,... | collective-permute-start | bytes 4423688 | tf_op jit(solution)/shard_map/ppermute | solution.py:813
  194.3 37.3 %collective-permute-start.13 = (bf16[2,1,2,2,1,24,3072]{6,5,4,3,2,1,0:T(8,128)(2,1)}, bf16[2,1,2,2,1,24,3072]{6,5,4,3,2,1,0:T(8,128)(2,1)S(1)}, u32[]{:S(2)}, u32[]{:S(2)}) collective-permute-start(bf16[2,1,2,2,1,24,3072]{6,5,4,3,2,1,0:T(8,128)(2,1)} %get-tuple-element.117), channel_id=1, source_target_pairs={{0,1},{1,0},{2,3},{3,2},{4,5},{5,4},{6,7},{7,6},{8,9},{9,8},{10,11... | collective-permute-start | bytes 3538952 | tf_op jit(solution)/shard_map/ppermute | solution.py:813
  231.6 1.0 copy-start.11
  231.6 1.5 copy-start.3
  237.8 18.6 %collective-permute-start.23 = (bf16[1,1,2,2,1,24,3840]{6,5,4,3,2,1,0:T(8,128)(2,1)}, bf16[1,1,2,2,1,24,3840]{6,5,4,3,2,1,0:T(8,128)(2,1)S(1)}, u32[]{:S(2)}, u32[]{:S(2)}) collective-permute-start(bf16[1,1,2,2,1,24,3840]{6,5,4,3,2,1,0:T(8,128)(2,1)} %get-tuple-element.126), channel_id=1, source_target_pairs={{0,1},{1,0},{2,3},{3,2},{4,5},{5,4},{6,7},{7,6},{8,9},{9,8},{10,11... | collective-permute-start | bytes 2211848 | tf_op jit(solution)/shard_map/ppermute | solution.py:813
  238.9 15.2 %collective-permute-start.24 = (bf16[1,1,2,2,1,24,3072]{6,5,4,3,2,1,0:T(8,128)(2,1)}, bf16[1,1,2,2,1,24,3072]{6,5,4,3,2,1,0:T(8,128)(2,1)}, u32[]{:S(2)}, u32[]{:S(2)}) collective-permute-start(bf16[1,1,2,2,1,24,3072]{6,5,4,3,2,1,0:T(8,128)(2,1)} %get-tuple-element.127), channel_id=1, source_target_pairs={{0,16},{1,17},{2,18},{3,19},{4,20},{5,21},{6,22},{7,23},{8,24},{9,... | collective-permute-start | bytes 1769480 | tf_op jit(solution)/shard_map/ppermute | solution.py:813
  253.0 4.9 %copy-start.12 = (bf16[2,1,2,2,1,24,3072]{6,5,4,3,2,1,0:T(8,128)(2,1)S(1)}, bf16[2,1,2,2,1,24,3072]{6,5,4,3,2,1,0:T(8,128)(2,1)}, u32[]{:S(2)}) copy-start(bf16[2,1,2,2,1,24,3072]{6,5,4,3,2,1,0:T(8,128)(2,1)} %copy-done.11) | copy-start | bytes 3538948
  253.0 11.3 %collective-permute-start.14 = (bf16[384,2560]{1,0:T(8,128)(2,1)}, bf16[384,2560]{1,0:T(8,128)(2,1)}, u32[]{:S(2)}, u32[]{:S(2)}) collective-permute-start(bf16[384,2560]{1,0:T(8,128)(2,1)} %get-tuple-element.121), channel_id=1, source_target_pairs={{0,8},{1,9},{2,10},{3,11},{4,12},{5,13},{6,14},{7,15},{8,0},{9,1},... | collective-permute-start | bytes 5898248 | tf_op jit(solution)/shard_map/ppermute | solution.py:813
  256.4 0.8 copy-start.9
  257.9 4.6 %copy-start.4 = (bf16[1,1,2,2,2,24,3840]{6,5,4,3,2,1,0:T(8,128)(2,1)S(1)}, bf16[1,1,2,2,2,24,3840]{6,5,4,3,2,1,0:T(8,128)(2,1)}, u32[]{:S(2)}) copy-start(bf16[1,1,2,2,2,24,3840]{6,5,4,3,2,1,0:T(8,128)(2,1)} %copy-done.3) | copy-start | bytes 4423684
  257.9 4.6 %copy-start.10 = (bf16[1,1,2,2,1,24,3840]{6,5,4,3,2,1,0:T(8,128)(2,1)S(1)}, bf16[1,1,2,2,1,24,3840]{6,5,4,3,2,1,0:T(8,128)(2,1)}, u32[]{:S(2)}) copy-start(bf16[1,1,2,2,1,24,3840]{6,5,4,3,2,1,0:T(8,128)(2,1)} %get-tuple-element.129) | copy-start | bytes 2211844
  259.9 22.0 %collective-permute-start.26 = (bf16[1,1,2,1,1,24,3072]{6,5,4,3,2,1,0:T(8,128)(2,1)S(1)}, bf16[1,1,2,1,1,24,3072]{6,5,4,3,2,1,0:T(8,128)(2,1)}, u32[]{:S(2)}, u32[]{:S(2)}) collective-permute-start(bf16[1,1,2,1,1,24,3072]{6,5,4,3,2,1,0:T(8,128)(2,1)S(1)} %dynamic-slice_convert_fusion.3), channel_id=1, source_target_pairs={{0,2},{1,3},{2,0},{3,1},{4,6},{5,7},{6,4},{7,5},{8,10},{9,11},{10,... | collective-permute-start | bytes 884744 | tf_op jit(solution)/shard_map/ppermute | solution.py:813
  262.5 2.0 copy-start.14
  266.6 12.5 %collective-permute-start.19 = (bf16[2,1,2,2,1,24,1280]{6,5,4,3,2,1,0:T(8,128)(2,1)S(1)}, bf16[2,1,2,2,1,24,1280]{6,5,4,3,2,1,0:T(8,128)(2,1)S(1)}, u32[]{:S(2)}, u32[]{:S(2)}) collective-permute-start(bf16[2,1,2,2,1,24,1280]{6,5,4,3,2,1,0:T(8,128)(2,1)S(1)} %dynamic-slice_convert_fusion), channel_id=1, source_target_pairs={{0,1},{1,0},{2,3},{3,2},{4,5},{5,4},{6,7},{7,6},{8,9},{9,8},{10,11... | collective-permute-start | bytes 1474568 | tf_op jit(solution)/shard_map/ppermute | solution.py:813
  267.3 14.6 %collective-permute-start.25 = (bf16[1,1,2,1,1,24,3840]{6,5,4,3,2,1,0:T(8,128)(2,1)S(1)}, bf16[1,1,2,1,1,24,3840]{6,5,4,3,2,1,0:T(8,128)(2,1)S(1)}, u32[]{:S(2)}, u32[]{:S(2)}) collective-permute-start(bf16[1,1,2,1,1,24,3840]{6,5,4,3,2,1,0:T(8,128)(2,1)S(1)} %dynamic-slice_convert_fusion.2), channel_id=1, source_target_pairs={{0,2},{1,3},{2,0},{3,1},{4,6},{5,7},{6,4},{7,5},{8,10},{9,11},{10,... | collective-permute-start | bytes 1105928 | tf_op jit(solution)/shard_map/ppermute | solution.py:813
  267.5 12.4 %collective-permute-start.15 = (bf16[1,1,2,2,2,24,1280]{6,5,4,3,2,1,0:T(8,128)(2,1)S(1)}, bf16[1,1,2,2,2,24,1280]{6,5,4,3,2,1,0:T(8,128)(2,1)S(1)}, u32[]{:S(2)}, u32[]{:S(2)}) collective-permute-start(bf16[1,1,2,2,2,24,1280]{6,5,4,3,2,1,0:T(8,128)(2,1)S(1)} %dynamic-slice_convert_fusion.1), channel_id=1, source_target_pairs={{0,16},{1,17},{2,18},{3,19},{4,20},{5,21},{6,22},{7,23},{8,24},{9,... | collective-permute-start | bytes 1474568 | tf_op jit(solution)/shard_map/ppermute | solution.py:813
  279.2 1.0 copy-start.5
  279.3 1.0 copy-start.18
  279.3 9.1 %collective-permute-start.20 = (bf16[1,1,2,2,1,24,1280]{6,5,4,3,2,1,0:T(8,128)(2,1)S(1)}, bf16[1,1,2,2,1,24,1280]{6,5,4,3,2,1,0:T(8,128)(2,1)}, u32[]{:S(2)}, u32[]{:S(2)}) collective-permute-start(bf16[1,1,2,2,1,24,1280]{6,5,4,3,2,1,0:T(8,128)(2,1)S(1)} %dynamic-slice_convert_fusion.4.refs_3_), channel_id=1, source_target_pairs={{0,16},{1,17},{2,18},{3,19},{4,20},{5,21},{6,22},{7,23},{8,24},{9,... | collective-permute-start | bytes 737288 | tf_op jit(solution)/shard_map/ppermute | solution.py:813
  280.2 1.0 copy-start.7
  281.2 0.7 copy-start.19
  281.2 11.5 %collective-permute-start.16 = (bf16[1,1,2,2,1,24,1280]{6,5,4,3,2,1,0:T(8,128)(2,1)S(1)}, bf16[1,1,2,2,1,24,1280]{6,5,4,3,2,1,0:T(8,128)(2,1)}, u32[]{:S(2)}, u32[]{:S(2)}) collective-permute-start(bf16[1,1,2,2,1,24,1280]{6,5,4,3,2,1,0:T(8,128)(2,1)S(1)} %dynamic-slice_convert_fusion.5.refs_2_), channel_id=1, source_target_pairs={{0,1},{1,0},{2,3},{3,2},{4,5},{5,4},{6,7},{7,6},{8,9},{9,8},{10,11... | collective-permute-start | bytes 737288 | tf_op jit(solution)/shard_map/ppermute | solution.py:813
  281.9 0.7 copy-start.15
  282.6 4.0 %copy-start.16 = (bf16[1,1,2,1,1,24,3840]{6,5,4,3,2,1,0:T(8,128)(2,1)S(1)}, bf16[1,1,2,1,1,24,3840]{6,5,4,3,2,1,0:T(8,128)(2,1)}, u32[]{:S(2)}) copy-start(bf16[1,1,2,1,1,24,3840]{6,5,4,3,2,1,0:T(8,128)(2,1)} %get-tuple-element.131) | copy-start | bytes 1105924
  283.7 21.4 %collective-permute-start.28 = (bf16[1,1,1,1,1,24,3072]{6,5,4,3,2,1,0:T(8,128)(2,1)S(1)}, bf16[1,1,1,1,1,24,3072]{6,5,4,3,2,1,0:T(8,128)(2,1)S(1)}, u32[]{:S(2)}, u32[]{:S(2)}) collective-permute-start(bf16[1,1,1,1,1,24,3072]{6,5,4,3,2,1,0:T(8,128)(2,1)S(1)} %dynamic-slice_convert_fusion.7), channel_id=1, source_target_pairs={{0,4},{1,5},{2,6},{3,7},{4,0},{5,1},{6,2},{7,3},{8,12},{9,13},{10,... | collective-permute-start | bytes 442376 | tf_op jit(solution)/shard_map/ppermute | solution.py:813
  286.6 1.8 copy-start.6
  286.7 5.9 %copy-start.8 = (f32[1,1,2,2,2,24,1280]{6,5,4,3,2,1,0:T(8,128)S(1)}, f32[1,1,2,2,2,24,1280]{6,5,4,3,2,1,0:T(8,128)}, u32[]{:S(2)}) copy-start(f32[1,1,2,2,2,24,1280]{6,5,4,3,2,1,0:T(8,128)} %copy-done.7) | copy-start | bytes 2949124
  286.7 18.4 %collective-permute-start.27 = (bf16[1,1,1,1,1,24,3840]{6,5,4,3,2,1,0:T(8,128)(2,1)S(1)}, bf16[1,1,1,1,1,24,3840]{6,5,4,3,2,1,0:T(8,128)(2,1)S(1)}, u32[]{:S(2)}, u32[]{:S(2)}) collective-permute-start(bf16[1,1,1,1,1,24,3840]{6,5,4,3,2,1,0:T(8,128)(2,1)S(1)} %dynamic-slice_convert_fusion.6), channel_id=1, source_target_pairs={{0,4},{1,5},{2,6},{3,7},{4,0},{5,1},{6,2},{7,3},{8,12},{9,13},{10,... | collective-permute-start | bytes 552968 | tf_op jit(solution)/shard_map/ppermute | solution.py:813
  289.4 9.4 %collective-permute-start.21 = (bf16[1,1,2,1,1,24,1280]{6,5,4,3,2,1,0:T(8,128)(2,1)S(1)}, bf16[1,1,2,1,1,24,1280]{6,5,4,3,2,1,0:T(8,128)(2,1)S(1)}, u32[]{:S(2)}, u32[]{:S(2)}) collective-permute-start(bf16[1,1,2,1,1,24,1280]{6,5,4,3,2,1,0:T(8,128)(2,1)S(1)} %dynamic-slice_convert_fusion.8), channel_id=1, source_target_pairs={{0,2},{1,3},{2,0},{3,1},{4,6},{5,7},{6,4},{7,5},{8,10},{9,11},{10,... | collective-permute-start | bytes 368648 | tf_op jit(solution)/shard_map/ppermute | solution.py:813
  293.7 10.0 %collective-permute-start.17 = (bf16[1,1,2,1,1,24,1280]{6,5,4,3,2,1,0:T(8,128)(2,1)S(1)}, bf16[1,1,2,1,1,24,1280]{6,5,4,3,2,1,0:T(8,128)(2,1)S(1)}, u32[]{:S(2)}, u32[]{:S(2)}) collective-permute-start(bf16[1,1,2,1,1,24,1280]{6,5,4,3,2,1,0:T(8,128)(2,1)S(1)} %dynamic-slice_convert_fusion.9), channel_id=1, source_target_pairs={{0,2},{1,3},{2,0},{3,1},{4,6},{5,7},{6,4},{7,5},{8,10},{9,11},{10,... | collective-permute-start | bytes 368648 | tf_op jit(solution)/shard_map/ppermute | solution.py:813
  298.9 6.2 %copy-start.23 = (bf16[1,1,1,1,1,24,1280]{6,5,4,3,2,1,0:T(8,128)(2,1)}, bf16[1,1,1,1,1,24,1280]{6,5,4,3,2,1,0:T(8,128)(2,1)S(1)}, u32[]{:S(2)}) copy-start(bf16[1,1,1,1,1,24,1280]{6,5,4,3,2,1,0:T(8,128)(2,1)S(1)} %dynamic-slice_convert_fusion.10.refs_3_) | copy-start | bytes 184324
  298.9 10.0 %collective-permute-start.22 = (bf16[1,1,1,1,1,24,1280]{6,5,4,3,2,1,0:T(8,128)(2,1)S(1)}, bf16[1,1,1,1,1,24,1280]{6,5,4,3,2,1,0:T(8,128)(2,1)S(1)}, u32[]{:S(2)}, u32[]{:S(2)}) collective-permute-start(bf16[1,1,1,1,1,24,1280]{6,5,4,3,2,1,0:T(8,128)(2,1)S(1)} %dynamic-slice_convert_fusion.10.refs_3_), channel_id=1, source_target_pairs={{0,4},{1,5},{2,6},{3,7},{4,0},{5,1},{6,2},{7,3},{8,12},{9,13},{10,... | collective-permute-start | bytes 184328 | tf_op jit(solution)/shard_map/ppermute | solution.py:813
  303.7 1.4 copy-start.24
  303.7 5.3 %collective-permute-start.18 = (bf16[1,1,1,1,1,24,1280]{6,5,4,3,2,1,0:T(8,128)(2,1)S(1)}, bf16[1,1,1,1,1,24,1280]{6,5,4,3,2,1,0:T(8,128)(2,1)S(1)}, u32[]{:S(2)}, u32[]{:S(2)}) collective-permute-start(bf16[1,1,1,1,1,24,1280]{6,5,4,3,2,1,0:T(8,128)(2,1)S(1)} %dynamic-slice_convert_fusion.11.refs_2_), channel_id=1, source_target_pairs={{0,4},{1,5},{2,6},{3,7},{4,0},{5,1},{6,2},{7,3},{8,12},{9,13},{10,... | collective-permute-start | bytes 184328 | tf_op jit(solution)/shard_map/ppermute | solution.py:813
  305.1 0.7 copy-start.22
  305.8 0.7 copy-start.20
  309.0 0.6 copy-start.25
  309.0 0.6 copy-start.26
Sparse Core Ops, SparseCore 0:
  11.0 93.5 all-gather.3
  239.6 57.7 all-gather.5

commit v2 on v1

--- a/solution.py
+++ b/solution.py
@@ -213,7 +213,7 @@
             parts.append(dot(soft, values))
         lane = lane_iota((TOK, 128))
         att_ref[:, at : at + 128] = jnp.where(lane < HD, parts[0], parts[1]).astype(bf16)
-    branch_ref[...] = dot(att_ref[...], two_ref[:, D:]) + vec_ref[2:3, :]
+    branch_ref[...] = (dot(att_ref[...], two_ref[:, D:]) + vec_ref[2:3, :]).astype(bf16)
 
 
 def backward_kernel(packed_ref, soft_ref, att_ref, gbr_ref, two_ref, table_ref, hot_ref, *refs):
@@ -617,7 +617,7 @@
             shaped((WINDOWS * TOK, 3 * D), bf16),
             shaped((WINDOWS * HEADS, TOK, TOK), bf16),
             shaped((WINDOWS * TOK, D), bf16),
-            shaped((WINDOWS * TOK, D), f32),
+            shaped((WINDOWS * TOK, D), bf16),
             shaped((16, D), f32),
             shaped((D, 128 + 2 * D), bf16),
             shaped((D, 2 * D), bf16),
@@ -1024,7 +1024,7 @@
         start += windows
     gpacked = [b[0] for b in back]
     image_grad, sums1, tables, flag = end(image, gbr, one, two, vec, gpacked, [b[2] for b in back], flag)
-    feed, flag = links.narrow(feed, (first[1], second[1]), (FF + D, FF), [flag])
+    feed, flag = links.narrow(feed, (first[1], second[1]), ((FF + D) // 2, FF // 2), [flag])
     all_tables = lax.all_gather(tables, AXES, axis=0, tiled=False)
     gin_k, gin_s, flag = attention_weights(core, (sums1, sums2, gupb), tiles, gpacked, [b[1] for b in back], flag)
     recv = links.tie([f[0][-1] for f in feed], [flag])

time: 321 us -> 319 us (level)
  no operation moved by 1% of the time
where the time goes in v2:
time: 319 us; the launch traced here: 318 us
  Pallas kernels  189 us (59%)
  waiting for transfers between devices  39.3 us (12%)
  starting transfers between devices  30.4 us (10%)
  local copies, waits for them, and re-layouts  20.3 us (6%)
  other arithmetic  20.3 us (6%)
  between operations  18.1 us (6%)
    pallas_call x1, Pallas kernels, middle(): pl.pallas_call(middle_kernel, grid=(steps + 1,), out_shape=(shaped((GH, G...  67.6 us
    ppermute x29, waiting for transfers between devices, swap(): return lax.ppermute(value, AXES, [(i, i ^ bit) for i in range(self.count)])  39.2 us
    pallas_call x2, Pallas kernels, backward(): pl.pallas_call(backward_kernel, grid=(count,), out_shape=(shaped((count *...  31.9 us
    pallas_call x1, Pallas kernels, forward(): pl.pallas_call(forward_kernel, grid=(WINDOWS,), out_shape=(shaped((WINDOW...  31.5 us
    ppermute x29, starting transfers between devices, swap(): return lax.ppermute(value, AXES, [(i, i ^ bit) for i in range(self.count)])  30.3 us
    pallas_call x1, Pallas kernels, end(): pl.pallas_call(end_kernel, out_shape=(shaped((GH, GW, D), bf16), shaped((...  16.1 us
    pallas_call x1, Pallas kernels, attention_weights(): pl.pallas_call(attention_weights_kernel, grid=(1,), out_shape=(shaped((D...  13.5 us
    unnamed x62, local copies, waits for them, and re-layouts  11.3 us
  transfers between devices with their start and end apart: 31, of which 11 were waited for; matrix products, arithmetic and copies ran while one was open for 10% of the time, Pallas kernels for 34%

profile of v2, /device:TPU:0, one launch (start us, length us, event | category | flops | bytes accessed | tf_op | source)
XLA Modules:
  0.0 317.5 jit_solution(991937185321864928)
XLA Ops:
  7.3 1.9 pack_feed.1
  9.3 0.8 slice.15
  10.0 0.8 fusion.12
  10.8 4.1 %collective-permute-start = (bf16[1,1,1,1,1,24,1536]{6,5,4,3,2,1,0:T(8,128)(2,1)S(1)}, bf16[1,1,1,1,1,24,1536]{6,5,4,3,2,1,0:T(8,128)(2,1)S(1)}, u32[]{:S(2)}, u32[]{:S(2)}) collective-permute-start(bf16[1,1,1,1,1,24,1536]{6,5,4,3,2,1,0:T(8,128)(2,1)S(1)} %get-tuple-element.163), channel_id=1, source_target_pairs={{0,4},{1,5},{2,6},{3,7},{4,0},{5,1},{6,2},{7,3},{8,12},{9,13},{10,... | collective-permute-start | bytes 221192 | tf_op jit(solution)/shard_map/ppermute | solution.py:813
  14.9 1.4 stack.53.eight_ref
  16.3 1.7 pack.1
  18.0 1.5 copy.61
  19.5 0.8 copy.62
  20.4 0.8 copy.67.valid_ref
  21.9 1.9 collective-permute-start.1
  23.8 1.1 collective-permute-done.2
  25.0 1.0 fusion.7
  26.3 5.0 %collective-permute-done.1 = bf16[1,1,2,1,1,24,1536]{6,5,2,4,3,1,0:T(8,128)(2,1)S(1)} collective-permute-done((bf16[1,1,2,1,1,24,1536]{6,5,2,4,3,1,0:T(8,128)(2,1)S(1)}, bf16[1,1,2,1,1,24,1536]{6,5,2,4,3,1,0:T(8,128)(2,1)S(1)}, u32[]{:S(2)}, u32[]{:S(2)}) %collective-permute-start.1) | collective-permute-done | bytes 147488 | tf_op jit(solution)/shard_map/ppermute | solution.py:813
  32.8 1.6 collective-permute-start.4
  34.4 1.9 collective-permute-done.3
  36.4 1.6 collective-permute-start.5
  38.1 0.7 copy.69.refs_1_
  38.9 4.9 %weigh.1 = (f32[992,768]{1,0:T(8,128)}, bf16[992,768]{1,0:T(8,128)(2,1)}, bf16[128,256]{1,0:T(8,128)(2,1)}, bf16[128,256]{1,0:T(8,128)(2,1)}, s32[1]{0:T(128)}) custom-call(s32[1]{0:T(128)S(6)} %copy.88.count_ref, bf16[26,38,768]{2,1,0:T(8,128)(2,1)} %bitcast.131, s32[300,2]{1,0:T(8,128)} %bitcast.140, s32[300,2]{1,0:T(8,128)} %bitcast.141, ...), custom_call_target="tpu_custom_call" | custom-call | flops 30000000 | bytes 6000000 | tf_op jit(solution)/shard_map/weigh/pallas_call | solution.py:593
  45.1 0.8 maximum_select_fusion.5
  46.1 1.7 collective-permute-start.6
  47.9 1.2 collective-permute-start.7
  49.1 1.2 fusion.6
  50.3 4.9 %begin.1 = (f32[84,16,768]{2,1,0:T(8,128)}, s32[1]{0:T(128)}) custom-call(bf16[26,38,768]{2,1,0:T(8,128)(2,1)} %bitcast.121, bf16[2,1,2,2,1,24,1536]{6,5,4,3,2,1,0:T(8,128)(2,1)} %copy-done.1, bf16[1,1,2,2,2,24,1664]{6,5,4,3,2,1,0:T(8,128)(2,1)} %copy-done.13), custom_call_target="tpu_custom_call" | custom-call | flops 30000000 | bytes 6000000 | tf_op jit(solution)/shard_map/begin/pallas_call | solution.py:581
  56.5 1.3 fusion.4
  57.8 5.7 %collective-permute-done.6 = bf16[1,1,2,2,2,24,1664]{6,5,4,3,2,1,0:T(8,128)(2,1)S(1)} collective-permute-done((bf16[1,1,2,2,2,24,1664]{6,5,4,3,2,1,0:T(8,128)(2,1)S(1)}, bf16[1,1,2,2,2,24,1664]{6,5,4,3,2,1,0:T(8,128)(2,1)S(1)}, u32[]{:S(2)}, u32[]{:S(2)}) %collective-permute-start.6) | collective-permute-done | bytes 639008 | tf_op jit(solution)/shard_map/ppermute | solution.py:813
  63.5 1.3 maximum_select_fusion.1
  64.8 2.0 collective-permute-done.7
  66.8 2.9 fusion.1
  70.3 1.3 maximum_select_fusion.refs_0_
  71.6 1.2 collective-permute-done.9
  72.8 1.0 copy-done.29
  73.8 31.5 %attend.1 = (bf16[1344,768]{1,0:T(8,128)(2,1)}, bf16[1344,2304]{1,0:T(8,128)(2,1)}, bf16[72,224,224]{2,1,0:T(8,128)(2,1)}, bf16[1344,768]{1,0:T(8,128)(2,1)}, bf...) custom-call(s32[5]{0:T(128)} %stack.59.places_ref.places, ...), custom_call_target="tpu_custom_call" | custom-call | flops 30000001024 | bytes 28000000 | tf_op jit(solution)/shard_map/attend/pallas_call | solution.py:612
  105.3 67.6 %feed.1 = (bf16[26,38,768]{2,1,0:T(8,128)(2,1)}, bf16[84,16,768]{2,1,0:T(8,128)(2,1)}, bf16[384,3840]{1,0:T(8,128)(2,1)}, bf16[384,3840]{1,0:T(8,128)(2,1)}, bf1...) custom-call(s32[1]{0:T(128)} %bitcast.core_ref, ...), custom_call_target="tpu_custom_call" | custom-call | flops 49999998976 | bytes 36000000 | tf_op jit(solution)/shard_map/feed/pallas_call | solution.py:646
  173.6 11.8 %attend_back.2 = (bf16[448,2304]{1,0:T(8,128)(2,1)}, f32[8,768]{1,0:T(8,128)}, f32[256,128]{1,0:T(8,128)}, s32[1]{0:T(128)}) custom-call(bf16[1344,2304]{1,0:T(8,128)(2,1)} %get-tuple-element.95.packed_ref, bf16[72,224,224]{2,1,0:T(8,128)(2,1)} %get-tuple-element.96.soft_ref, bf16[1344,768]{1,0:T(8,128)(2,1)} %get-tuple-element.90.refs_1_.att_ref, ...), custom_call_target="tpu_custom_call" | custom-call | flops 1000000000 | bytes 2000000 | tf_op jit(solution)/shard_map/attend_back/pallas_call | solution.py:699
  185.4 1.6 copy-done
  187.0 5.2 %narrow.2 = (bf16[1,1,2,2,2,24,3840]{6,5,4,3,2,1,0:T(8,128)(2,1)}, bf16[2,1,2,2,1,24,3072]{6,5,4,3,2,1,0:T(8,128)(2,1)}, s32[1]{0:T(128)}) custom-call(s32[5]{0:T(128)} %stack.59.places_ref.places, bf16[2,1,2,2,2,24,3840]{6,5,4,3,2,1,0:T(8,128)(2,1)} %bitcast.112, bf16[2,1,2,2,2,24,3840]{6,5,4,3,2,1,0:T(8,128)(2,1)} %bitcast.115, ...), custom_call_target="tpu_custom_call" | custom-call | flops 5308416 | bytes 10616832 | tf_op jit(solution)/shard_map/narrow/pallas_call | solution.py:921
  192.2 1.6 collective-permute-start.12
  193.7 1.1 collective-permute-start.13
  194.9 20.1 %attend_back.3 = (bf16[896,2304]{1,0:T(8,128)(2,1)}, f32[8,768]{1,0:T(8,128)}, f32[256,128]{1,0:T(8,128)}, s32[1]{0:T(128)}) custom-call(bf16[1344,2304]{1,0:T(8,128)(2,1)} %get-tuple-element.95.packed_ref, bf16[72,224,224]{2,1,0:T(8,128)(2,1)} %get-tuple-element.96.soft_ref, bf16[1344,768]{1,0:T(8,128)(2,1)} %get-tuple-element.90.refs_1_.att_ref, ...), custom_call_target="tpu_custom_call" | custom-call | flops 1000000000 | bytes 2000000 | tf_op jit(solution)/shard_map/attend_back/pallas_call | solution.py:699
  215.0 16.1 %end.1 = (bf16[26,38,768]{2,1,0:T(8,128)(2,1)}, f32[8,768]{1,0:T(8,128)}, f32[64,128]{1,0:T(8,128)}, s32[1]{0:T(128)}) custom-call(bf16[26,38,768]{2,1,0:T(8,128)(2,1)} %bitcast.123, bf16[84,16,768]{2,1,0:T(8,128)(2,1)} %get-tuple-element.92.gbr_ref, bf16[768,1664]{1,0:T(8,128)(2,1)} %get-tuple-element.93.one_ref, ...), custom_call_target="tpu_custom_call" | custom-call | flops 1000000000 | bytes 2000000 | tf_op jit(solution)/shard_map/end/pallas_call | solution.py:746
  231.1 1.0 copy-done.11
  232.6 4.6 %narrow.3 = (bf16[1,1,2,2,1,24,3840]{6,5,4,3,2,1,0:T(8,128)(2,1)}, bf16[1,1,2,2,1,24,3072]{6,5,4,3,2,1,0:T(8,128)(2,1)}, s32[1]{0:T(128)}) custom-call(s32[5]{0:T(128)} %stack.59.places_ref.places, bf16[2,1,2,2,2,24,3840]{6,5,4,3,2,1,0:T(8,128)(2,1)} %bitcast.113, bf16[2,1,2,2,2,24,3840]{6,5,4,3,2,1,0:T(8,128)(2,1)} %bitcast.116, ...), custom_call_target="tpu_custom_call" | custom-call | flops 2654208 | bytes 5308416 | tf_op jit(solution)/shard_map/narrow/pallas_call | solution.py:921
  237.1 0.9 collective-permute-start.23
  238.5 13.5 %attend_weights.1 = (bf16[384,2560]{1,0:T(8,128)(2,1)}, bf16[384,2560]{1,0:T(8,128)(2,1)}, s32[1]{0:T(128)}) custom-call(s32[1]{0:T(128)} %bitcast.core_ref, f32[8,768]{1,0:T(8,128)} %get-tuple-element.110.sums1_ref, f32[8,768]{1,0:T(8,128)} %get-tuple-element.111.sums2_ref, f32[8,768]{1,0:T(8,128)} %get-tuple-element.112.gupb_ref, ...), custom_call_target="tpu_custom_call" | custom-call | flops 1000000000 | bytes 2000000 | tf_op jit(solution)/shard_map/attend_weights/pallas_call | solution.py:727
  252.1 1.1 collective-permute-done.24.refs_1_
  253.2 2.4 collective-permute-done.23.refs_0_
  255.6 0.9 copy-done.9
  257.1 1.9 convert_add_fusion.3
  259.1 2.4 collective-permute-start.26
  261.4 1.8 convert_add_fusion.2
  263.4 2.1 convert_add_fusion
  267.0 11.1 %collective-permute-done.19 = bf16[2,1,2,2,1,24,1280]{6,5,4,3,2,1,0:T(8,128)(2,1)S(1)} collective-permute-done((bf16[2,1,2,2,1,24,1280]{6,5,4,3,2,1,0:T(8,128)(2,1)S(1)}, bf16[2,1,2,2,1,24,1280]{6,5,4,3,2,1,0:T(8,128)(2,1)S(1)}, u32[]{:S(2)}, u32[]{:S(2)}) %collective-permute-start.19) | collective-permute-done | bytes 491552 | tf_op jit(solution)/shard_map/ppermute | solution.py:813
  279.2 0.9 copy-done.7
  281.6 1.1 convert_add_fusion.7
  282.7 2.9 collective-permute-start.28
  285.9 0.8 dynamic-slice_bitcast_fusion.refs_0_
  287.4 1.0 convert_add_fusion.8
  288.4 3.3 %collective-permute-start.21 = (bf16[1,1,2,1,1,24,1280]{6,5,4,3,2,1,0:T(8,128)(2,1)S(1)}, bf16[1,1,2,1,1,24,1280]{6,5,4,3,2,1,0:T(8,128)(2,1)S(1)}, u32[]{:S(2)}, u32[]{:S(2)}) collective-permute-start(bf16[1,1,2,1,1,24,1280]{6,5,4,3,2,1,0:T(8,128)(2,1)S(1)} %dynamic-slice_convert_fusion.8), channel_id=1, source_target_pairs={{0,2},{1,3},{2,0},{3,1},{4,6},{5,7},{6,4},{7,5},{8,10},{9,11},{10,... | collective-permute-start | bytes 368648 | tf_op jit(solution)/shard_map/ppermute | solution.py:813
  291.7 1.0 convert_add_fusion.9
  292.9 5.0 %collective-permute-done.21 = bf16[1,1,2,1,1,24,1280]{6,5,4,3,2,1,0:T(8,128)(2,1)S(1)} collective-permute-done((bf16[1,1,2,1,1,24,1280]{6,5,4,3,2,1,0:T(8,128)(2,1)S(1)}, bf16[1,1,2,1,1,24,1280]{6,5,4,3,2,1,0:T(8,128)(2,1)S(1)}, u32[]{:S(2)}, u32[]{:S(2)}) %collective-permute-start.21) | collective-permute-done | bytes 122912 | tf_op jit(solution)/shard_map/ppermute | solution.py:813
  297.9 1.7 collective-permute-start.22
  299.7 2.6 collective-permute-done.17
  305.1 2.5 unpack_feed.1
  308.3 2.2 unpack_in.1
  (133 shorter events, 14.3 us)
Async XLA Ops:
  7.2 12.4 %copy-start.27 = (s32[1,300,2]{1,2,0:T(2,128)S(1)}, s32[1,300,2]{1,2,0:T(2,128)}, u32[]{:S(2)}) copy-start(s32[1,300,2]{1,2,0:T(2,128)} %param.26) | copy-start | bytes 7204
  7.2 13.2 %copy-start.28 = (s32[1,300]{1,0:T(1,128)S(1)}, s32[1,300]{1,0:T(1,128)}, u32[]{:S(2)}) copy-start(s32[1,300]{1,0:T(1,128)} %param.27) | copy-start | bytes 3604
  7.2 98.1 %all-gather.4.cloned.1.call-start = ((), (), s32[]{:S(2)}) async-start(), calls=%async_computation | async-start | bytes 9732096 | tf_op jit(solution)/shard_map/all_gather | solution.py:993
  9.2 298.4 %all-gather.6.cloned.1.call-start = ((), (), s32[]{:S(2)}) async-start(), calls=%async_computation.1 | async-start | bytes 1081344 | tf_op jit(solution)/shard_map/all_gather | solution.py:1028
  10.8 11.0 %collective-permute-start = (bf16[1,1,1,1,1,24,1536]{6,5,4,3,2,1,0:T(8,128)(2,1)S(1)}, bf16[1,1,1,1,1,24,1536]{6,5,4,3,2,1,0:T(8,128)(2,1)S(1)}, u32[]{:S(2)}, u32[]{:S(2)}) collective-permute-start(bf16[1,1,1,1,1,24,1536]{6,5,4,3,2,1,0:T(8,128)(2,1)S(1)} %get-tuple-element.163), channel_id=1, source_target_pairs={{0,4},{1,5},{2,6},{3,7},{4,0},{5,1},{6,2},{7,3},{8,12},{9,13},{10,... | collective-permute-start | bytes 221192 | tf_op jit(solution)/shard_map/ppermute | solution.py:813
  18.0 8.3 %copy-start.21 = (bf16[24,1664]{1,0:T(8,128)(2,1)S(1)}, bf16[24,1664]{1,0:T(8,128)(2,1)}, u32[]{:S(2)}) copy-start(bf16[24,1664]{1,0:T(8,128)(2,1)} %pack.1) | copy-start | bytes 239620
  18.0 6.9 %collective-permute-start.2 = (bf16[1,1,1,1,1,24,1664]{6,5,4,3,2,1,0:T(8,128)(2,1)}, bf16[1,1,1,1,1,24,1664]{6,5,4,3,2,1,0:T(8,128)(2,1)S(1)}, u32[]{:S(2)}, u32[]{:S(2)}) collective-permute-start(bf16[1,1,1,1,1,24,1664]{6,5,4,3,2,1,0:T(8,128)(2,1)} %bitcast.137), channel_id=1, source_target_pairs={{0,4},{1,5},{2,6},{3,7},{4,0},{5,1},{6,2},{7,3},{8,12},{9,13},{10,... | collective-permute-start | bytes 239624 | tf_op jit(solution)/shard_map/ppermute | solution.py:813
  21.9 9.5 %collective-permute-start.1 = (bf16[1,1,2,1,1,24,1536]{6,5,2,4,3,1,0:T(8,128)(2,1)S(1)}, bf16[1,1,2,1,1,24,1536]{6,5,2,4,3,1,0:T(8,128)(2,1)S(1)}, u32[]{:S(2)}, u32[]{:S(2)}) collective-permute-start(bf16[1,1,2,1,1,24,1536]{6,5,2,4,3,1,0:T(8,128)(2,1)S(1)} %fusion.8), channel_id=1, source_target_pairs={{0,2},{1,3},{2,0},{3,1},{4,6},{5,7},{6,4},{7,5},{8,10},{9,11},{10,... | collective-permute-start | bytes 442376 | tf_op jit(solution)/shard_map/ppermute | solution.py:813
  26.0 10.4 %collective-permute-start.3 = (bf16[1,1,2,1,1,24,1664]{6,5,2,4,3,1,0:T(8,128)(2,1)S(1)}, bf16[1,1,2,1,1,24,1664]{6,5,2,4,3,1,0:T(8,128)(2,1)S(1)}, u32[]{:S(2)}, u32[]{:S(2)}) collective-permute-start(bf16[1,1,2,1,1,24,1664]{6,5,2,4,3,1,0:T(8,128)(2,1)S(1)} %fusion.7), channel_id=1, source_target_pairs={{0,2},{1,3},{2,0},{3,1},{4,6},{5,7},{6,4},{7,5},{8,10},{9,11},{10,... | collective-permute-start | bytes 479240 | tf_op jit(solution)/shard_map/ppermute | solution.py:813
  32.8 15.0 %collective-permute-start.4 = (bf16[1,1,2,2,1,24,1536]{6,5,3,2,4,1,0:T(8,128)(2,1)}, bf16[1,1,2,2,1,24,1536]{6,5,3,2,4,1,0:T(8,128)(2,1)S(1)}, u32[]{:S(2)}, u32[]{:S(2)}) collective-permute-start(bf16[1,1,2,2,1,24,1536]{6,5,3,2,4,1,0:T(8,128)(2,1)} %copy.70), channel_id=1, source_target_pairs={{0,16},{1,17},{2,18},{3,19},{4,20},{5,21},{6,22},{7,23},{8,24},{9,... | collective-permute-start | bytes 884744 | tf_op jit(solution)/shard_map/ppermute | solution.py:813
  36.4 9.4 %collective-permute-start.5 = (bf16[1,1,2,2,1,24,1664]{6,5,2,3,4,1,0:T(8,128)(2,1)S(1)}, bf16[1,1,2,2,1,24,1664]{6,5,2,3,4,1,0:T(8,128)(2,1)S(1)}, u32[]{:S(2)}, u32[]{:S(2)}) collective-permute-start(bf16[1,1,2,2,1,24,1664]{6,5,2,3,4,1,0:T(8,128)(2,1)S(1)} %maximum_select_fusion.3), channel_id=1, source_target_pairs={{0,1},{1,0},{2,3},{3,2},{4,5},{5,4},{6,7},{7,6},{8,9},{9,8},{10,11... | collective-permute-start | bytes 958472 | tf_op jit(solution)/shard_map/ppermute | solution.py:813
  46.1 4.2 %copy-start.13 = (bf16[1,1,2,2,2,24,1664]{6,5,4,3,2,1,0:T(8,128)(2,1)}, bf16[1,1,2,2,2,24,1664]{6,5,4,3,2,1,0:T(8,128)(2,1)S(1)}, u32[]{:S(2)}) copy-start(bf16[1,1,2,2,2,24,1664]{6,5,4,3,2,1,0:T(8,128)(2,1)S(1)} %copy_select_fusion.refs_1_) | copy-start | bytes 1916932
  46.1 17.4 %collective-permute-start.6 = (bf16[1,1,2,2,2,24,1664]{6,5,4,3,2,1,0:T(8,128)(2,1)S(1)}, bf16[1,1,2,2,2,24,1664]{6,5,4,3,2,1,0:T(8,128)(2,1)S(1)}, u32[]{:S(2)}, u32[]{:S(2)}) collective-permute-start(bf16[1,1,2,2,2,24,1664]{6,5,4,3,2,1,0:T(8,128)(2,1)S(1)} %copy_select_fusion.refs_1_), channel_id=1, source_target_pairs={{0,16},{1,17},{2,18},{3,19},{4,20},{5,21},{6,22},{7,23},{8,24},{9,... | collective-permute-start | bytes 1916936 | tf_op jit(solution)/shard_map/ppermute | solution.py:813
  47.8 1.3 copy-start.17
  47.9 2.4 copy-start.1
  47.9 18.9 %collective-permute-start.7 = (bf16[2,1,2,2,1,24,1536]{6,5,4,3,2,1,0:T(8,128)(2,1)S(1)}, bf16[2,1,2,2,1,24,1536]{6,5,4,3,2,1,0:T(8,128)(2,1)}, u32[]{:S(2)}, u32[]{:S(2)}) collective-permute-start(bf16[2,1,2,2,1,24,1536]{6,5,4,3,2,1,0:T(8,128)(2,1)S(1)} %fusion.5.refs_0_), channel_id=1, source_target_pairs={{0,1},{1,0},{2,3},{3,2},{4,5},{5,4},{6,7},{7,6},{8,9},{9,8},{10,11... | collective-permute-start | bytes 1769480 | tf_op jit(solution)/shard_map/ppermute | solution.py:813
  57.8 9.0 %copy-start.2 = (bf16[2,1,2,2,1,24,1536]{6,5,4,3,2,1,0:T(8,128)(2,1)S(1)}, bf16[2,1,2,2,1,24,1536]{6,5,4,3,2,1,0:T(8,128)(2,1)}, u32[]{:S(2)}) copy-start(bf16[2,1,2,2,1,24,1536]{6,5,4,3,2,1,0:T(8,128)(2,1)} %copy-done.1) | copy-start | bytes 1769476
  64.8 8.0 %collective-permute-start.8 = (bf16[2,1,2,2,2,24,1664]{6,5,4,3,2,1,0:T(8,128)(2,1)}, bf16[2,1,2,2,2,24,1664]{6,5,4,3,2,1,0:T(8,128)(2,1)}, u32[]{:S(2)}, u32[]{:S(2)}) collective-permute-start(bf16[2,1,2,2,2,24,1664]{6,5,4,3,2,1,0:T(8,128)(2,1)} %maximum_select_fusion.1), channel_id=1, source_target_pairs={{0,8},{1,9},{2,10},{3,11},{4,12},{5,13},{6,14},{7,15},{8,0},{9,1},... | collective-permute-start | bytes 3833864 | tf_op jit(solution)/shard_map/ppermute | solution.py:813
  69.7 3.1 collective-permute-start.9
  72.8 1.0 copy-start.29
  173.0 12.4 %collective-permute-start.10 = (bf16[384,3840]{1,0:T(8,128)(2,1)}, bf16[384,3840]{1,0:T(8,128)(2,1)S(1)}, u32[]{:S(2)}, u32[]{:S(2)}) collective-permute-start(bf16[384,3840]{1,0:T(8,128)(2,1)} %get-tuple-element.100), channel_id=1, source_target_pairs={{0,8},{1,9},{2,10},{3,11},{4,12},{5,13},{6,14},{7,15},{8,0},{9,1},... | collective-permute-start | bytes 8847368 | tf_op jit(solution)/shard_map/ppermute | solution.py:813
  173.2 12.2 %collective-permute-start.11 = (bf16[384,3072]{1,0:T(8,128)(2,1)}, bf16[384,3072]{1,0:T(8,128)(2,1)}, u32[]{:S(2)}, u32[]{:S(2)}) collective-permute-start(bf16[384,3072]{1,0:T(8,128)(2,1)} %get-tuple-element.102), channel_id=1, source_target_pairs={{0,8},{1,9},{2,10},{3,11},{4,12},{5,13},{6,14},{7,15},{8,0},{9,1},... | collective-permute-start | bytes 7077896 | tf_op jit(solution)/shard_map/ppermute | solution.py:813
  185.4 1.6 copy-start
  192.2 38.9 %collective-permute-start.12 = (bf16[1,1,2,2,2,24,3840]{6,5,4,3,2,1,0:T(8,128)(2,1)}, bf16[1,1,2,2,2,24,3840]{6,5,4,3,2,1,0:T(8,128)(2,1)S(1)}, u32[]{:S(2)}, u32[]{:S(2)}) collective-permute-start(bf16[1,1,2,2,2,24,3840]{6,5,4,3,2,1,0:T(8,128)(2,1)} %get-tuple-element.116), channel_id=1, source_target_pairs={{0,16},{1,17},{2,18},{3,19},{4,20},{5,21},{6,22},{7,23},{8,24},{9,... | collective-permute-start | bytes 4423688 | tf_op jit(solution)/shard_map/ppermute | solution.py:813
  193.7 37.3 %collective-permute-start.13 = (bf16[2,1,2,2,1,24,3072]{6,5,4,3,2,1,0:T(8,128)(2,1)}, bf16[2,1,2,2,1,24,3072]{6,5,4,3,2,1,0:T(8,128)(2,1)S(1)}, u32[]{:S(2)}, u32[]{:S(2)}) collective-permute-start(bf16[2,1,2,2,1,24,3072]{6,5,4,3,2,1,0:T(8,128)(2,1)} %get-tuple-element.117), channel_id=1, source_target_pairs={{0,1},{1,0},{2,3},{3,2},{4,5},{5,4},{6,7},{7,6},{8,9},{9,8},{10,11... | collective-permute-start | bytes 3538952 | tf_op jit(solution)/shard_map/ppermute | solution.py:813
  231.1 1.0 copy-start.11
  231.1 1.5 copy-start.3
  237.1 18.5 %collective-permute-start.23 = (bf16[1,1,2,2,1,24,3840]{6,5,4,3,2,1,0:T(8,128)(2,1)}, bf16[1,1,2,2,1,24,3840]{6,5,4,3,2,1,0:T(8,128)(2,1)S(1)}, u32[]{:S(2)}, u32[]{:S(2)}) collective-permute-start(bf16[1,1,2,2,1,24,3840]{6,5,4,3,2,1,0:T(8,128)(2,1)} %get-tuple-element.126), channel_id=1, source_target_pairs={{0,1},{1,0},{2,3},{3,2},{4,5},{5,4},{6,7},{7,6},{8,9},{9,8},{10,11... | collective-permute-start | bytes 2211848 | tf_op jit(solution)/shard_map/ppermute | solution.py:813
  238.0 15.1 %collective-permute-start.24 = (bf16[1,1,2,2,1,24,3072]{6,5,4,3,2,1,0:T(8,128)(2,1)}, bf16[1,1,2,2,1,24,3072]{6,5,4,3,2,1,0:T(8,128)(2,1)}, u32[]{:S(2)}, u32[]{:S(2)}) collective-permute-start(bf16[1,1,2,2,1,24,3072]{6,5,4,3,2,1,0:T(8,128)(2,1)} %get-tuple-element.127), channel_id=1, source_target_pairs={{0,16},{1,17},{2,18},{3,19},{4,20},{5,21},{6,22},{7,23},{8,24},{9,... | collective-permute-start | bytes 1769480 | tf_op jit(solution)/shard_map/ppermute | solution.py:813
  252.0 5.1 %copy-start.12 = (bf16[2,1,2,2,1,24,3072]{6,5,4,3,2,1,0:T(8,128)(2,1)S(1)}, bf16[2,1,2,2,1,24,3072]{6,5,4,3,2,1,0:T(8,128)(2,1)}, u32[]{:S(2)}) copy-start(bf16[2,1,2,2,1,24,3072]{6,5,4,3,2,1,0:T(8,128)(2,1)} %copy-done.11) | copy-start | bytes 3538948
  252.0 11.2 %collective-permute-start.14 = (bf16[384,2560]{1,0:T(8,128)(2,1)}, bf16[384,2560]{1,0:T(8,128)(2,1)}, u32[]{:S(2)}, u32[]{:S(2)}) collective-permute-start(bf16[384,2560]{1,0:T(8,128)(2,1)} %get-tuple-element.121), channel_id=1, source_target_pairs={{0,8},{1,9},{2,10},{3,11},{4,12},{5,13},{6,14},{7,15},{8,0},{9,1},... | collective-permute-start | bytes 5898248 | tf_op jit(solution)/shard_map/ppermute | solution.py:813
  255.6 0.9 copy-start.9
  257.1 4.3 %copy-start.4 = (bf16[1,1,2,2,2,24,3840]{6,5,4,3,2,1,0:T(8,128)(2,1)S(1)}, bf16[1,1,2,2,2,24,3840]{6,5,4,3,2,1,0:T(8,128)(2,1)}, u32[]{:S(2)}) copy-start(bf16[1,1,2,2,2,24,3840]{6,5,4,3,2,1,0:T(8,128)(2,1)} %copy-done.3) | copy-start | bytes 4423684
  257.1 4.3 %copy-start.10 = (bf16[1,1,2,2,1,24,3840]{6,5,4,3,2,1,0:T(8,128)(2,1)S(1)}, bf16[1,1,2,2,1,24,3840]{6,5,4,3,2,1,0:T(8,128)(2,1)}, u32[]{:S(2)}) copy-start(bf16[1,1,2,2,1,24,3840]{6,5,4,3,2,1,0:T(8,128)(2,1)} %get-tuple-element.129) | copy-start | bytes 2211844
  259.1 21.8 %collective-permute-start.26 = (bf16[1,1,2,1,1,24,3072]{6,5,4,3,2,1,0:T(8,128)(2,1)S(1)}, bf16[1,1,2,1,1,24,3072]{6,5,4,3,2,1,0:T(8,128)(2,1)}, u32[]{:S(2)}, u32[]{:S(2)}) collective-permute-start(bf16[1,1,2,1,1,24,3072]{6,5,4,3,2,1,0:T(8,128)(2,1)S(1)} %dynamic-slice_convert_fusion.3), channel_id=1, source_target_pairs={{0,2},{1,3},{2,0},{3,1},{4,6},{5,7},{6,4},{7,5},{8,10},{9,11},{10,... | collective-permute-start | bytes 884744 | tf_op jit(solution)/shard_map/ppermute | solution.py:813
  261.4 2.0 copy-start.14
  265.6 12.5 %collective-permute-start.19 = (bf16[2,1,2,2,1,24,1280]{6,5,4,3,2,1,0:T(8,128)(2,1)S(1)}, bf16[2,1,2,2,1,24,1280]{6,5,4,3,2,1,0:T(8,128)(2,1)S(1)}, u32[]{:S(2)}, u32[]{:S(2)}) collective-permute-start(bf16[2,1,2,2,1,24,1280]{6,5,4,3,2,1,0:T(8,128)(2,1)S(1)} %dynamic-slice_convert_fusion), channel_id=1, source_target_pairs={{0,1},{1,0},{2,3},{3,2},{4,5},{5,4},{6,7},{7,6},{8,9},{9,8},{10,11... | collective-permute-start | bytes 1474568 | tf_op jit(solution)/shard_map/ppermute | solution.py:813
  266.1 14.7 %collective-permute-start.25 = (bf16[1,1,2,1,1,24,3840]{6,5,4,3,2,1,0:T(8,128)(2,1)S(1)}, bf16[1,1,2,1,1,24,3840]{6,5,4,3,2,1,0:T(8,128)(2,1)S(1)}, u32[]{:S(2)}, u32[]{:S(2)}) collective-permute-start(bf16[1,1,2,1,1,24,3840]{6,5,4,3,2,1,0:T(8,128)(2,1)S(1)} %dynamic-slice_convert_fusion.2), channel_id=1, source_target_pairs={{0,2},{1,3},{2,0},{3,1},{4,6},{5,7},{6,4},{7,5},{8,10},{9,11},{10,... | collective-permute-start | bytes 1105928 | tf_op jit(solution)/shard_map/ppermute | solution.py:813
  266.4 12.4 %collective-permute-start.15 = (bf16[1,1,2,2,2,24,1280]{6,5,4,3,2,1,0:T(8,128)(2,1)S(1)}, bf16[1,1,2,2,2,24,1280]{6,5,4,3,2,1,0:T(8,128)(2,1)S(1)}, u32[]{:S(2)}, u32[]{:S(2)}) collective-permute-start(bf16[1,1,2,2,2,24,1280]{6,5,4,3,2,1,0:T(8,128)(2,1)S(1)} %dynamic-slice_convert_fusion.1), channel_id=1, source_target_pairs={{0,16},{1,17},{2,18},{3,19},{4,20},{5,21},{6,22},{7,23},{8,24},{9,... | collective-permute-start | bytes 1474568 | tf_op jit(solution)/shard_map/ppermute | solution.py:813
  278.2 1.0 copy-start.5
  278.3 1.0 copy-start.18
  278.3 9.1 %collective-permute-start.20 = (bf16[1,1,2,2,1,24,1280]{6,5,4,3,2,1,0:T(8,128)(2,1)S(1)}, bf16[1,1,2,2,1,24,1280]{6,5,4,3,2,1,0:T(8,128)(2,1)}, u32[]{:S(2)}, u32[]{:S(2)}) collective-permute-start(bf16[1,1,2,2,1,24,1280]{6,5,4,3,2,1,0:T(8,128)(2,1)S(1)} %dynamic-slice_convert_fusion.4.refs_3_), channel_id=1, source_target_pairs={{0,16},{1,17},{2,18},{3,19},{4,20},{5,21},{6,22},{7,23},{8,24},{9,... | collective-permute-start | bytes 737288 | tf_op jit(solution)/shard_map/ppermute | solution.py:813
  279.2 1.0 copy-start.7
  280.1 0.7 copy-start.19
  280.1 11.6 %collective-permute-start.16 = (bf16[1,1,2,2,1,24,1280]{6,5,4,3,2,1,0:T(8,128)(2,1)S(1)}, bf16[1,1,2,2,1,24,1280]{6,5,4,3,2,1,0:T(8,128)(2,1)}, u32[]{:S(2)}, u32[]{:S(2)}) collective-permute-start(bf16[1,1,2,2,1,24,1280]{6,5,4,3,2,1,0:T(8,128)(2,1)S(1)} %dynamic-slice_convert_fusion.5.refs_2_), channel_id=1, source_target_pairs={{0,1},{1,0},{2,3},{3,2},{4,5},{5,4},{6,7},{7,6},{8,9},{9,8},{10,11... | collective-permute-start | bytes 737288 | tf_op jit(solution)/shard_map/ppermute | solution.py:813
  280.9 0.7 copy-start.15
  281.6 4.0 %copy-start.16 = (bf16[1,1,2,1,1,24,3840]{6,5,4,3,2,1,0:T(8,128)(2,1)S(1)}, bf16[1,1,2,1,1,24,3840]{6,5,4,3,2,1,0:T(8,128)(2,1)}, u32[]{:S(2)}) copy-start(bf16[1,1,2,1,1,24,3840]{6,5,4,3,2,1,0:T(8,128)(2,1)} %get-tuple-element.131) | copy-start | bytes 1105924
  282.7 21.1 %collective-permute-start.28 = (bf16[1,1,1,1,1,24,3072]{6,5,4,3,2,1,0:T(8,128)(2,1)S(1)}, bf16[1,1,1,1,1,24,3072]{6,5,4,3,2,1,0:T(8,128)(2,1)S(1)}, u32[]{:S(2)}, u32[]{:S(2)}) collective-permute-start(bf16[1,1,1,1,1,24,3072]{6,5,4,3,2,1,0:T(8,128)(2,1)S(1)} %dynamic-slice_convert_fusion.7), channel_id=1, source_target_pairs={{0,4},{1,5},{2,6},{3,7},{4,0},{5,1},{6,2},{7,3},{8,12},{9,13},{10,... | collective-permute-start | bytes 442376 | tf_op jit(solution)/shard_map/ppermute | solution.py:813
  285.6 1.8 copy-start.6
  285.7 6.0 %copy-start.8 = (f32[1,1,2,2,2,24,1280]{6,5,4,3,2,1,0:T(8,128)S(1)}, f32[1,1,2,2,2,24,1280]{6,5,4,3,2,1,0:T(8,128)}, u32[]{:S(2)}) copy-start(f32[1,1,2,2,2,24,1280]{6,5,4,3,2,1,0:T(8,128)} %copy-done.7) | copy-start | bytes 2949124
  285.7 18.1 %collective-permute-start.27 = (bf16[1,1,1,1,1,24,3840]{6,5,4,3,2,1,0:T(8,128)(2,1)S(1)}, bf16[1,1,1,1,1,24,3840]{6,5,4,3,2,1,0:T(8,128)(2,1)S(1)}, u32[]{:S(2)}, u32[]{:S(2)}) collective-permute-start(bf16[1,1,1,1,1,24,3840]{6,5,4,3,2,1,0:T(8,128)(2,1)S(1)} %dynamic-slice_convert_fusion.6), channel_id=1, source_target_pairs={{0,4},{1,5},{2,6},{3,7},{4,0},{5,1},{6,2},{7,3},{8,12},{9,13},{10,... | collective-permute-start | bytes 552968 | tf_op jit(solution)/shard_map/ppermute | solution.py:813
  288.4 9.4 %collective-permute-start.21 = (bf16[1,1,2,1,1,24,1280]{6,5,4,3,2,1,0:T(8,128)(2,1)S(1)}, bf16[1,1,2,1,1,24,1280]{6,5,4,3,2,1,0:T(8,128)(2,1)S(1)}, u32[]{:S(2)}, u32[]{:S(2)}) collective-permute-start(bf16[1,1,2,1,1,24,1280]{6,5,4,3,2,1,0:T(8,128)(2,1)S(1)} %dynamic-slice_convert_fusion.8), channel_id=1, source_target_pairs={{0,2},{1,3},{2,0},{3,1},{4,6},{5,7},{6,4},{7,5},{8,10},{9,11},{10,... | collective-permute-start | bytes 368648 | tf_op jit(solution)/shard_map/ppermute | solution.py:813
  292.8 9.5 %collective-permute-start.17 = (bf16[1,1,2,1,1,24,1280]{6,5,4,3,2,1,0:T(8,128)(2,1)S(1)}, bf16[1,1,2,1,1,24,1280]{6,5,4,3,2,1,0:T(8,128)(2,1)S(1)}, u32[]{:S(2)}, u32[]{:S(2)}) collective-permute-start(bf16[1,1,2,1,1,24,1280]{6,5,4,3,2,1,0:T(8,128)(2,1)S(1)} %dynamic-slice_convert_fusion.9), channel_id=1, source_target_pairs={{0,2},{1,3},{2,0},{3,1},{4,6},{5,7},{6,4},{7,5},{8,10},{9,11},{10,... | collective-permute-start | bytes 368648 | tf_op jit(solution)/shard_map/ppermute | solution.py:813
  297.9 5.9 %copy-start.23 = (bf16[1,1,1,1,1,24,1280]{6,5,4,3,2,1,0:T(8,128)(2,1)}, bf16[1,1,1,1,1,24,1280]{6,5,4,3,2,1,0:T(8,128)(2,1)S(1)}, u32[]{:S(2)}) copy-start(bf16[1,1,1,1,1,24,1280]{6,5,4,3,2,1,0:T(8,128)(2,1)S(1)} %dynamic-slice_convert_fusion.10.refs_3_) | copy-start | bytes 184324
  297.9 9.7 %collective-permute-start.22 = (bf16[1,1,1,1,1,24,1280]{6,5,4,3,2,1,0:T(8,128)(2,1)S(1)}, bf16[1,1,1,1,1,24,1280]{6,5,4,3,2,1,0:T(8,128)(2,1)S(1)}, u32[]{:S(2)}, u32[]{:S(2)}) collective-permute-start(bf16[1,1,1,1,1,24,1280]{6,5,4,3,2,1,0:T(8,128)(2,1)S(1)} %dynamic-slice_convert_fusion.10.refs_3_), channel_id=1, source_target_pairs={{0,4},{1,5},{2,6},{3,7},{4,0},{5,1},{6,2},{7,3},{8,12},{9,13},{10,... | collective-permute-start | bytes 184328 | tf_op jit(solution)/shard_map/ppermute | solution.py:813
  302.4 1.4 copy-start.24
  302.4 5.3 %collective-permute-start.18 = (bf16[1,1,1,1,1,24,1280]{6,5,4,3,2,1,0:T(8,128)(2,1)S(1)}, bf16[1,1,1,1,1,24,1280]{6,5,4,3,2,1,0:T(8,128)(2,1)S(1)}, u32[]{:S(2)}, u32[]{:S(2)}) collective-permute-start(bf16[1,1,1,1,1,24,1280]{6,5,4,3,2,1,0:T(8,128)(2,1)S(1)} %dynamic-slice_convert_fusion.11.refs_2_), channel_id=1, source_target_pairs={{0,4},{1,5},{2,6},{3,7},{4,0},{5,1},{6,2},{7,3},{8,12},{9,13},{10,... | collective-permute-start | bytes 184328 | tf_op jit(solution)/shard_map/ppermute | solution.py:813
  303.8 0.7 copy-start.22
  304.5 0.7 copy-start.20
  307.6 0.6 copy-start.25
  307.6 0.6 copy-start.26
Sparse Core Ops, SparseCore 0:
  11.0 93.9 all-gather.3
  238.7 59.9 all-gather.5
